TPU v7x, 32 devices: a whole 2x2x4 slice. The times are simulated.
32 devices in a mesh: dp: 2 (over y), expert: 16 (over z, x, core).
Axes of the slice: x: 2, y: 2, z: 4, core: 2. Of those that a mesh axis runs over, the one named last changes fastest.
Arguments:
- tokens: bfloat16 [512, 4096], P('expert', 'dp'), may hold values from -6 to 6
- expert_ids: int32 [512, 8], P('expert'), may hold values from 0 to 15, all different within a row; in each aligned block of 32 rows (0 to 31, 32 to 63, ...) at most 32 rows name the same one
- route_weights: float32 [512, 8], P('expert'), may hold values from 0.05 to 0.3
- cotangent: bfloat16 [512, 4096], P('expert', 'dp'), may hold values from -6 to 6
- w_gate: bfloat16 [16, 4096, 1536], P('expert', 'dp'), may hold values from -0.09375 to 0.09375
- w_up: bfloat16 [16, 4096, 1536], P('expert', 'dp'), may hold values from -0.09375 to 0.09375
- w_down: bfloat16 [16, 1536, 4096], P('expert', None, 'dp'), may hold values from -0.15625 to 0.15625
Outputs:
- mixed: bfloat16 [512, 4096], P('expert', 'dp')
- token_grad: bfloat16 [512, 4096], P('expert', 'dp')
- down_grad: bfloat16 [16, 1536, 4096], P('expert', None, 'dp')
Inputs may be any that keep to these rules, and one draw needn't show every extreme that they name: `expert_ids`: each row names 8 different experts. Among the 32 rows of one token group no expert is named more than 32 times, a bound that some block reaches.
All inputs are finite; a program needn't handle non-finite values.
Results may differ from a plain program's by a relative error of at most 0.015.
Values may be sent and summed in bfloat16 or wider, within the bound.
A program may use at most 128 MiB of HBM per device.

v0:
```python
import jax
import jax.numpy as jnp
from jax import lax
from jax.sharding import PartitionSpec as P


def pointwise(gate_pre, up_pre, grad_hidden):
    sigmoid_g = jax.nn.sigmoid(gate_pre)
    activation = gate_pre * sigmoid_g
    hidden = (activation * up_pre).astype(jnp.bfloat16)
    slope = sigmoid_g * (1.0 + gate_pre * (1.0 - sigmoid_g))
    grad_gate = (grad_hidden * up_pre * slope).astype(jnp.bfloat16)
    grad_up = (grad_hidden * activation).astype(jnp.bfloat16)
    return (hidden, grad_gate, grad_up)


def split_sums(full_sums, hidden_width):
    return pointwise(
        full_sums[:, :hidden_width],
        full_sums[:, hidden_width : 2 * hidden_width],
        full_sums[:, 2 * hidden_width :],
    )


def shards(tokens, expert_ids, route_weights, cotangent, w_gate, w_up, w_down):
    tok_rows, feat_width = tokens.shape
    top_count = expert_ids.shape[1]
    expert_count = lax.axis_size("expert")
    capacity = min(tok_rows, 2 * tok_rows * top_count // expert_count)
    slots_total = expert_count * capacity
    pair_count = tok_rows * top_count
    flat_ids = expert_ids.reshape(pair_count)
    onehot = (flat_ids[:, None] == jnp.arange(expert_count, dtype=jnp.int32)[None, :]).astype(
        jnp.int32
    )
    position = jnp.sum((jnp.cumsum(onehot, axis=0) - onehot) * onehot, axis=1)
    slot_index = flat_ids * capacity + position
    chosen = slot_index[:, None] == jnp.arange(slots_total, dtype=jnp.int32)[None, :]
    chosen_b = chosen.astype(jnp.bfloat16)
    x_pairs = jnp.repeat(tokens, top_count, axis=0)
    pair_weights = route_weights.reshape(pair_count, 1)
    dy_pairs = (jnp.repeat(cotangent, top_count, axis=0).astype(jnp.float32) * pair_weights).astype(
        jnp.bfloat16
    )
    contract_pairs = (((0,), (0,)), ((), ()))
    send_x = lax.dot_general(
        chosen_b, x_pairs, contract_pairs, preferred_element_type=jnp.float32
    ).astype(jnp.bfloat16)
    send_dy = lax.dot_general(
        chosen_b, dy_pairs, contract_pairs, preferred_element_type=jnp.float32
    ).astype(jnp.bfloat16)
    recv_x, recv_dy = (
        lax.all_to_all(
            send_x.reshape(expert_count, capacity, feat_width),
            "expert",
            split_axis=0,
            concat_axis=0,
            tiled=True,
        ),
        lax.all_to_all(
            send_dy.reshape(expert_count, capacity, feat_width),
            "expert",
            split_axis=0,
            concat_axis=0,
            tiled=True,
        ),
    )
    rows_x = recv_x.reshape(slots_total, feat_width)
    rows_dy = recv_dy.reshape(slots_total, feat_width)
    gate_local = w_gate[0]
    up_local = w_up[0]
    down_local = w_down[0]
    hidden_width = gate_local.shape[1]
    contract_last = (((1,), (1,)), ((), ()))
    gate_part = jnp.dot(rows_x, gate_local, preferred_element_type=jnp.float32)
    up_part = jnp.dot(rows_x, up_local, preferred_element_type=jnp.float32)
    back_part = lax.dot_general(
        rows_dy, down_local, contract_last, preferred_element_type=jnp.float32
    )
    row_share = lax.psum_scatter(
        jnp.concatenate([gate_part, up_part, back_part], axis=1).astype(jnp.bfloat16),
        "dp",
        scatter_dimension=0,
        tiled=True,
    ).astype(jnp.float32)
    hidden_s, gate_s, up_s = split_sums(row_share, hidden_width)
    hidden, grad_gate, grad_up = (
        lax.all_gather(hidden_s, "dp", axis=0, tiled=True),
        lax.all_gather(gate_s, "dp", axis=0, tiled=True),
        lax.all_gather(up_s, "dp", axis=0, tiled=True),
    )
    expert_out = jnp.dot(hidden, down_local, preferred_element_type=jnp.float32).astype(
        jnp.bfloat16
    )
    grad_rows = lax.dot_general(
        grad_gate, gate_local, contract_last, preferred_element_type=jnp.float32
    )
    grad_rows = (
        grad_rows
        + lax.dot_general(grad_up, up_local, contract_last, preferred_element_type=jnp.float32)
    ).astype(jnp.bfloat16)
    down_grad = lax.dot_general(
        hidden, rows_dy, contract_pairs, preferred_element_type=jnp.float32
    ).astype(jnp.bfloat16)
    back_out, back_grad = (
        lax.all_to_all(
            expert_out.reshape(expert_count, capacity, feat_width),
            "expert",
            split_axis=0,
            concat_axis=0,
            tiled=True,
        ),
        lax.all_to_all(
            grad_rows.reshape(expert_count, capacity, feat_width),
            "expert",
            split_axis=0,
            concat_axis=0,
            tiled=True,
        ),
    )
    weighted_sel = (
        (chosen.astype(jnp.float32) * pair_weights)
        .reshape(tok_rows, top_count, slots_total)
        .sum(axis=1)
    )
    plain_sel = chosen_b.reshape(tok_rows, top_count, slots_total).sum(axis=1)
    mixed = jnp.dot(
        weighted_sel,
        back_out.reshape(slots_total, feat_width).astype(jnp.float32),
        precision=lax.Precision.HIGHEST,
    ).astype(jnp.bfloat16)
    token_grad = jnp.dot(
        plain_sel, back_grad.reshape(slots_total, feat_width), preferred_element_type=jnp.float32
    ).astype(jnp.bfloat16)
    return (mixed, token_grad, down_grad[None])


def solution(mesh):
    return jax.shard_map(
        shards,
        mesh=mesh,
        in_specs=(
            P("expert", "dp"),
            P("expert", None),
            P("expert", None),
            P("expert", "dp"),
            P("expert", "dp", None),
            P("expert", "dp", None),
            P("expert", None, "dp"),
        ),
        out_specs=(P("expert", "dp"), P("expert", "dp"), P("expert", None, "dp")),
        check_vma=False,
    )
```

profile of v0, /device:TPU:11, one launch (start us, length us, event | category | flops | bytes accessed | tf_op | source)
XLA Modules:
  0.0 374.4 jit_solution(13125480844806655352)
XLA Ops:
  7.2 0.0 copy-start
  7.2 0.8 copy.18
  8.0 0.1 eq.50
  8.1 0.1 eq.46
  8.2 0.6 reduce-window.6
  8.8 0.2 slice_reduce_fusion
  9.0 0.1 fusion.40
  9.1 2.2 convolution_convert_fusion.2
  11.3 6.7 %all-to-all-start = ((bf16[16,32,2048]{2,1,0:T(8,128)(2,1)}), bf16[16,32,2048]{2,1,0:T(8,128)(2,1)S(1)}, u32[]{:S(2)}, u32[]{:S(2)}) async-start(bf16[16,32,2048]{2,1,0:T(8,128)(2,1)} %bitcast.2), calls=%async_computation | async-start | bytes 4194304 | tf_op jit(solution)/shard_map/all_to_all | solution.py:53
  18.0 0.1 copy.22
  18.0 0.1 mul.64
  18.2 2.2 convolution_convert_fusion.1
  20.4 45.0 %all-to-all-done = bf16[16,32,2048]{2,1,0:T(8,128)(2,1)S(1)} async-done(((bf16[16,32,2048]{2,1,0:T(8,128)(2,1)}), bf16[16,32,2048]{2,1,0:T(8,128)(2,1)S(1)}, u32[]{:S(2)}, u32[]{:S(2)}) %all-to-all-start) | async-done | bytes 2097184 | tf_op jit(solution)/shard_map/all_to_all | solution.py:53
  65.4 1.3 copy-done.3
  66.7 4.9 %all-to-all-start.1 = ((bf16[16,32,2048]{2,1,0:T(8,128)(2,1)}), bf16[16,32,2048]{2,1,0:T(8,128)(2,1)S(1)}, u32[]{:S(2)}, u32[]{:S(2)}) async-start(bf16[16,32,2048]{2,1,0:T(8,128)(2,1)} %bitcast.7), calls=%async_computation.1 | async-start | bytes 4194304 | tf_op jit(solution)/shard_map/all_to_all | solution.py:60
  71.6 0.0 reduce-scatter.2.cloned.1.call-start
  71.7 0.0 copy-start.4
  71.7 8.1 %fusion.15 = bf16[512,1536]{1,0:T(8,128)(2,1)} fusion(bf16[512,2048]{1,0:T(8,128)(2,1)} %bitcast.77, bf16[1,2048,1536]{2,1,0:T(8,128)(2,1)} %param.11), kind=kOutput, calls=%fused_computation.18 | convolution fusion | flops 3222011904 | bytes 9961472 | tf_op jit(solution)/shard_map/dot_general | solution.py:75
  79.8 7.3 %fusion.18 = bf16[512,1536]{1,0:T(8,128)(2,1)} fusion(bf16[512,2048]{1,0:T(8,128)(2,1)S(1)} %bitcast.78, bf16[1,2048,1536]{2,1,0:T(8,128)(2,1)} %param.12), kind=kOutput, calls=%fused_computation.19 | convolution fusion | flops 3222011904 | bytes 9961472 | tf_op jit(solution)/shard_map/dot_general | solution.py:76
  87.2 31.9 %all-to-all-done.1 = bf16[16,32,2048]{2,1,0:T(8,128)(2,1)S(1)} async-done(((bf16[16,32,2048]{2,1,0:T(8,128)(2,1)}), bf16[16,32,2048]{2,1,0:T(8,128)(2,1)S(1)}, u32[]{:S(2)}, u32[]{:S(2)}) %all-to-all-start.1) | async-done | bytes 2097184 | tf_op jit(solution)/shard_map/all_to_all | solution.py:60
  119.1 7.0 %fusion.21 = bf16[512,1536]{1,0:T(8,128)(2,1)S(1)} fusion(bf16[512,2048]{1,0:T(8,128)(2,1)S(1)} %bitcast.75, bf16[1,1536,2048]{2,1,0:T(8,128)(2,1)} %param.13), kind=kOutput, calls=%fused_computation.20 | convolution fusion | flops 3222011904 | bytes 9961472 | tf_op jit(solution)/shard_map/dot_general | solution.py:77
  126.1 2.4 pad_maximum_fusion
  128.5 0.0 reduce-scatter.2.cloned.1.call-update
  128.5 0.0 all-gather.8.cloned.1.call-start
  128.6 59.6 %reduce-scatter.2.cloned.1.call-done = bf16[256,4608]{1,0:T(8,128)(2,1)} async-done(((bf16[512,4608]{1,0:T(8,128)(2,1)}), bf16[256,4608]{1,0:T(8,128)(2,1)}) %reduce-scatter.2.cloned.1.call-update) | async-done | bytes 2359312 | tf_op jit(solution)/shard_map/reduce_scatter | solution.py:80
  188.2 2.2 convert_element_type.66
  190.4 2.4 multiply_convert_fusion.1
  192.8 0.0 all-gather.8.cloned.1.call-update
  192.8 0.2 all-gather.6.cloned.1.call-start
  193.1 0.5 all-gather.6.cloned.1.call-update
  193.6 26.6 %all-gather.8.cloned.1.call-done = bf16[512,1536]{1,0:T(8,128)(2,1)} async-done(((bf16[256,1536]{1,0:T(8,128)(2,1)}), bf16[512,1536]{1,0:T(8,128)(2,1)}) %all-gather.8.cloned.1.call-update) | async-done | bytes 1572880 | tf_op jit(solution)/shard_map/all_gather | solution.py:90
  220.2 8.7 %fusion.5 = f32[512,2048]{1,0:T(8,128)} fusion(bf16[512,1536]{1,0:T(8,128)(2,1)} %all-gather.8.cloned.1.call-done, bf16[1,2048,1536]{2,1,0:T(8,128)(2,1)} %param.12), kind=kOutput, calls=%fused_computation.6 | convolution fusion | flops 3221225472 | bytes 12058624 | tf_op jit(solution)/shard_map/dot_general | solution.py:100
  228.9 20.1 %all-gather.6.cloned.1.call-done = bf16[512,1536]{1,0:T(8,128)(2,1)} async-done(((bf16[256,1536]{1,0:T(8,128)(2,1)}), bf16[512,1536]{1,0:T(8,128)(2,1)}) %all-gather.6.cloned.1.call-update) | async-done | bytes 1572880 | tf_op jit(solution)/shard_map/all_gather | solution.py:89
  249.1 9.2 %add_convert_fusion = bf16[512,2048]{1,0:T(8,128)(2,1)} fusion(f32[512,2048]{1,0:T(8,128)} %fusion.5, bf16[512,1536]{1,0:T(8,128)(2,1)} %all-gather.6.cloned.1.call-done, bf16[1,2048,1536]{2,1,0:T(8,128)(2,1)} %param.11), kind=kOutput, calls=%fused_computation.15 | convolution fusion | flops 3223322624 | bytes 14155776 | tf_op jit(solution)/shard_map/dot_general | solution.py:95
  258.3 6.4 %all-to-all-start.3 = ((bf16[16,32,2048]{2,1,0:T(8,128)(2,1)}), bf16[16,32,2048]{2,1,0:T(8,128)(2,1)S(1)}, u32[]{:S(2)}, u32[]{:S(2)}) async-start(bf16[16,32,2048]{2,1,0:T(8,128)(2,1)} %bitcast.80), calls=%async_computation.4 | async-start | bytes 4194304 | tf_op jit(solution)/shard_map/all_to_all | solution.py:113
  264.7 0.0 all-gather.4.cloned.1.call-start
  264.7 0.5 all-gather.4.cloned.1.call-update
  265.3 28.5 %all-gather.4.cloned.1.call-done = bf16[512,1536]{1,0:T(8,128)(2,1)} async-done(((bf16[256,1536]{1,0:T(8,128)(2,1)}), bf16[512,1536]{1,0:T(8,128)(2,1)}) %all-gather.4.cloned.1.call-update) | async-done | bytes 1572880 | tf_op jit(solution)/shard_map/all_gather | solution.py:88
  293.7 8.0 %fusion.24 = bf16[512,2048]{1,0:T(8,128)(2,1)} fusion(bf16[512,1536]{1,0:T(8,128)(2,1)} %all-gather.4.cloned.1.call-done, bf16[1,1536,2048]{2,1,0:T(8,128)(2,1)} %param.13), kind=kOutput, calls=%fused_computation.21 | convolution fusion | flops 3222274048 | bytes 9961472 | tf_op jit(solution)/shard_map/dot_general | solution.py:92
  301.7 10.4 %all-to-all-done.3 = bf16[16,32,2048]{2,1,0:T(8,128)(2,1)S(1)} async-done(((bf16[16,32,2048]{2,1,0:T(8,128)(2,1)}), bf16[16,32,2048]{2,1,0:T(8,128)(2,1)S(1)}, u32[]{:S(2)}, u32[]{:S(2)}) %all-to-all-start.3) | async-done | bytes 2097184 | tf_op jit(solution)/shard_map/all_to_all | solution.py:113
  312.1 4.9 %all-to-all-start.2 = ((bf16[16,32,2048]{2,1,0:T(8,128)(2,1)}), bf16[16,32,2048]{2,1,0:T(8,128)(2,1)}, u32[]{:S(2)}, u32[]{:S(2)}) async-start(bf16[16,32,2048]{2,1,0:T(8,128)(2,1)} %bitcast.79), calls=%async_computation.3 | async-start | bytes 4194304 | tf_op jit(solution)/shard_map/all_to_all | solution.py:106
  317.0 0.1 reduce_sum.33
  317.1 0.2 fusion.35
  317.3 0.2 select_reduce_fusion
  317.6 8.2 %fusion = bf16[1,1536,2048]{2,1,0:T(8,128)(2,1)} fusion(bf16[512,1536]{1,0:T(8,128)(2,1)} %all-gather.4.cloned.1.call-done, bf16[512,2048]{1,0:T(8,128)(2,1)} %bitcast.76), kind=kOutput, calls=%fused_computation.1 | convolution fusion | flops 3224371200 | bytes 9961472 | tf_op jit(solution)/shard_map/dot_general | solution.py:102
  325.8 1.1 convolution_convert_fusion.3
  326.9 37.6 %all-to-all-done.2 = bf16[16,32,2048]{2,1,0:T(8,128)(2,1)} async-done(((bf16[16,32,2048]{2,1,0:T(8,128)(2,1)}), bf16[16,32,2048]{2,1,0:T(8,128)(2,1)}, u32[]{:S(2)}, u32[]{:S(2)}) %all-to-all-start.2) | async-done | bytes 2097184 | tf_op jit(solution)/shard_map/all_to_all | solution.py:106
  364.5 3.4 convolution_convert_fusion.4
  (21 shorter events, 0.1 us)
Async XLA Ops:
  7.2 1.9 copy-start
  11.3 6.7 %copy-start.8 = (f32[32,8]{0,1:T(8,128)S(1)}, f32[32,8]{0,1:T(8,128)}, u32[]{:S(2)}) copy-start(f32[32,8]{0,1:T(8,128)} %param.9) | copy-start | bytes 3076
  11.3 6.9 %copy-start.7 = (bf16[32,2048]{1,0:T(8,128)(2,1)S(1)}, bf16[32,2048]{1,0:T(8,128)(2,1)}, u32[]{:S(2)}) copy-start(bf16[32,2048]{1,0:T(8,128)(2,1)} %param.10) | copy-start | bytes 393220
  11.3 54.1 %all-to-all-start = ((bf16[16,32,2048]{2,1,0:T(8,128)(2,1)}), bf16[16,32,2048]{2,1,0:T(8,128)(2,1)S(1)}, u32[]{:S(2)}, u32[]{:S(2)}) async-start(bf16[16,32,2048]{2,1,0:T(8,128)(2,1)} %bitcast.2), calls=%async_computation | async-start | bytes 4194304 | tf_op jit(solution)/shard_map/all_to_all | solution.py:53
  65.4 1.3 copy-start.3
  66.7 52.3 %all-to-all-start.1 = ((bf16[16,32,2048]{2,1,0:T(8,128)(2,1)}), bf16[16,32,2048]{2,1,0:T(8,128)(2,1)S(1)}, u32[]{:S(2)}, u32[]{:S(2)}) async-start(bf16[16,32,2048]{2,1,0:T(8,128)(2,1)} %bitcast.7), calls=%async_computation.1 | async-start | bytes 4194304 | tf_op jit(solution)/shard_map/all_to_all | solution.py:60
  71.6 116.5 %reduce-scatter.2.cloned.1.call-start = ((), (), s32[]{:S(2)}) async-start(), calls=%async_computation.5 | async-start | bytes 7077888 | tf_op jit(solution)/shard_map/reduce_scatter | solution.py:80
  71.7 8.2 %copy-start.4 = (bf16[16,32,2048]{2,1,0:T(8,128)(2,1)S(1)}, bf16[16,32,2048]{2,1,0:T(8,128)(2,1)}, u32[]{:S(2)}) copy-start(bf16[16,32,2048]{2,1,0:T(8,128)(2,1)} %copy-done.3) | copy-start | bytes 6291460
  119.0 7.0 %copy-start.2 = (bf16[16,32,2048]{2,1,0:T(8,128)(2,1)}, bf16[16,32,2048]{2,1,0:T(8,128)(2,1)S(1)}, u32[]{:S(2)}) copy-start(bf16[16,32,2048]{2,1,0:T(8,128)(2,1)S(1)} %all-to-all-done.1) | copy-start | bytes 6291460
  119.0 7.1 %copy-start.5 = (bf16[512,1536]{1,0:T(8,128)(2,1)S(1)}, bf16[512,1536]{1,0:T(8,128)(2,1)}, u32[]{:S(2)}) copy-start(bf16[512,1536]{1,0:T(8,128)(2,1)} %fusion.15) | copy-start | bytes 4718596
  119.0 7.1 %copy-start.6 = (bf16[512,1536]{1,0:T(8,128)(2,1)S(1)}, bf16[512,1536]{1,0:T(8,128)(2,1)}, u32[]{:S(2)}) copy-start(bf16[512,1536]{1,0:T(8,128)(2,1)} %fusion.18) | copy-start | bytes 4718596
  128.5 91.7 %all-gather.8.cloned.1.call-start = ((), (), s32[]{:S(2)}) async-start(), calls=%async_computation.8 | async-start | bytes 2359296 | tf_op jit(solution)/shard_map/all_gather | solution.py:90
  192.8 56.2 %all-gather.6.cloned.1.call-start = ((), (), s32[]{:S(2)}) async-start(), calls=%async_computation.7 | async-start | bytes 2359296 | tf_op jit(solution)/shard_map/all_gather | solution.py:89
  258.3 53.8 %all-to-all-start.3 = ((bf16[16,32,2048]{2,1,0:T(8,128)(2,1)}), bf16[16,32,2048]{2,1,0:T(8,128)(2,1)S(1)}, u32[]{:S(2)}, u32[]{:S(2)}) async-start(bf16[16,32,2048]{2,1,0:T(8,128)(2,1)} %bitcast.80), calls=%async_computation.4 | async-start | bytes 4194304 | tf_op jit(solution)/shard_map/all_to_all | solution.py:113
  264.7 29.0 %all-gather.4.cloned.1.call-start = ((), (), s32[]{:S(2)}) async-start(), calls=%async_computation.6 | async-start | bytes 2359296 | tf_op jit(solution)/shard_map/all_gather | solution.py:88
  312.1 52.4 %all-to-all-start.2 = ((bf16[16,32,2048]{2,1,0:T(8,128)(2,1)}), bf16[16,32,2048]{2,1,0:T(8,128)(2,1)}, u32[]{:S(2)}, u32[]{:S(2)}) async-start(bf16[16,32,2048]{2,1,0:T(8,128)(2,1)} %bitcast.79), calls=%async_computation.3 | async-start | bytes 4194304 | tf_op jit(solution)/shard_map/all_to_all | solution.py:106
  325.8 42.1 %copy-start.1 = (bf16[32,2048]{1,0:T(8,128)(2,1)S(1)}, bf16[32,2048]{1,0:T(8,128)(2,1)}, u32[]{:S(2)}) copy-start(bf16[32,2048]{1,0:T(8,128)(2,1)} %param.7) | copy-start | bytes 393220
Sparse Core Ops, SparseCore 0:
  128.6 59.4 reduce-scatter.1
  192.9 27.1 all-gather.7
  221.8 27.2 all-gather.5
  266.8 26.8 all-gather.3
where the time goes:
time: 375 us; the launch traced here: 374 us
  waiting for transfers between devices  261 us (70%)
  matrix products  65.6 us (17%)
  starting transfers between devices  23.2 us (6%)
  between operations  13.9 us (4%)
  other arithmetic  8.2 us (2%)
    reduce_scatter x1, waiting for transfers between devices, shards(): lax.psum_scatter(jnp.concatenate([gate_part, up_part, back_part], axis=1)...  59.6 us
    all_to_all x1, waiting for transfers between devices, shards(): lax.all_to_all(send_x.reshape(expert_count, capacity, feat_width), 'exper...  45 us
    all_to_all x1, waiting for transfers between devices, shards(): lax.all_to_all(expert_out.reshape(expert_count, capacity, feat_width), 'e...  37.6 us
    all_to_all x1, waiting for transfers between devices, shards(): lax.all_to_all(send_dy.reshape(expert_count, capacity, feat_width), 'expe...  31.9 us
    all_gather x1, waiting for transfers between devices, shards(): lax.all_gather(hidden_s, 'dp', axis=0, tiled=True)  28.5 us
    all_gather x1, waiting for transfers between devices, shards(): lax.all_gather(up_s, 'dp', axis=0, tiled=True)  26.6 us
    all_gather x1, waiting for transfers between devices, shards(): lax.all_gather(gate_s, 'dp', axis=0, tiled=True)  20.1 us
    all_to_all x1, waiting for transfers between devices, shards(): lax.all_to_all(grad_rows.reshape(expert_count, capacity, feat_width), 'ex...  10.4 us
  transfers between devices with their start and end apart: 8, of which 8 were waited for; matrix products, arithmetic and copies ran while one was open for 12% of the time, Pallas kernels for 0%

commit v1 on v0

--- a/solution.py
+++ b/solution.py
@@ -22,7 +22,7 @@
     )
 
 
-def shards(tokens, expert_ids, route_weights, cotangent, w_gate, w_up, w_down):
+def shards_slots(tokens, expert_ids, route_weights, cotangent, w_gate, w_up, w_down):
     tok_rows, feat_width = tokens.shape
     top_count = expert_ids.shape[1]
     expert_count = lax.axis_size("expert")
@@ -133,6 +133,88 @@
         plain_sel, back_grad.reshape(slots_total, feat_width), preferred_element_type=jnp.float32
     ).astype(jnp.bfloat16)
     return (mixed, token_grad, down_grad[None])
+
+
+CHUNKS = 2
+
+
+def gather_rows(block):
+    return lax.all_gather(block, "expert", axis=0, tiled=True)
+
+
+def scatter_sum(rows):
+    parts = lax.all_to_all(
+        rows.reshape(lax.axis_size("expert"), -1, rows.shape[1]), "expert", 0, 0, tiled=True
+    )
+    return jnp.sum(parts.astype(jnp.float32), axis=0).astype(jnp.bfloat16)
+
+
+def swap_pieces(block):
+    return lax.ppermute(block, "dp", [(0, 1), (1, 0)])
+
+
+def shards_dense(tokens, expert_ids, route_weights, cotangent, w_gate, w_up, w_down):
+    tok_rows, feat_width = tokens.shape
+    expert_count = lax.axis_size("expert")
+    chunks = CHUNKS
+    step = tok_rows // chunks
+    me = lax.axis_index("expert")
+    named = expert_ids[:, :, None] == jnp.arange(expert_count, dtype=jnp.int32)[None, None, :]
+    dense = jnp.sum(jnp.where(named, route_weights[:, :, None], 0.0), axis=1)
+    all_weights = gather_rows(dense)
+    mine = lax.dynamic_slice_in_dim(all_weights, me, 1, axis=1).reshape(
+        expert_count, chunks, step
+    )
+    gate_local, up_local, down_local = w_gate[0], w_up[0], w_down[0]
+    last = (((1,), (1,)), ((), ()))
+    first = (((0,), (0,)), ((), ()))
+    f32 = jnp.float32
+    xs = [gather_rows(tokens[c * step : (c + 1) * step]) for c in range(chunks)]
+    cs = [gather_rows(cotangent[c * step : (c + 1) * step]) for c in range(chunks)]
+    ws = [mine[:, c, :].reshape(expert_count * step, 1) for c in range(chunks)]
+    hiddens, dys, mixed, token_grad = [], [], [], []
+    for c in range(chunks):
+        rows_x = xs[c]
+        gate_part = jnp.dot(rows_x, gate_local, preferred_element_type=f32).astype(jnp.bfloat16)
+        gate_other = swap_pieces(gate_part)
+        up_part = jnp.dot(rows_x, up_local, preferred_element_type=f32).astype(jnp.bfloat16)
+        up_other = swap_pieces(up_part)
+        rows_dy = (cs[c].astype(f32) * ws[c]).astype(jnp.bfloat16)
+        back_part = lax.dot_general(rows_dy, down_local, last, preferred_element_type=f32).astype(
+            jnp.bfloat16
+        )
+        back_other = swap_pieces(back_part)
+        hidden, grad_gate, grad_up = pointwise(
+            gate_part.astype(f32) + gate_other.astype(f32),
+            up_part.astype(f32) + up_other.astype(f32),
+            back_part.astype(f32) + back_other.astype(f32),
+        )
+        out = jnp.dot(hidden, down_local, preferred_element_type=f32)
+        mixed.append(scatter_sum((out * ws[c]).astype(jnp.bfloat16)))
+        grad = lax.dot_general(grad_gate, gate_local, last, preferred_element_type=f32)
+        grad = grad + lax.dot_general(grad_up, up_local, last, preferred_element_type=f32)
+        token_grad.append(scatter_sum(grad.astype(jnp.bfloat16)))
+        hiddens.append(hidden)
+        dys.append(rows_dy)
+    down_grad = lax.dot_general(
+        jnp.concatenate(hiddens, axis=0),
+        jnp.concatenate(dys, axis=0),
+        first,
+        preferred_element_type=f32,
+    ).astype(jnp.bfloat16)
+    return (
+        jnp.concatenate(mixed, axis=0),
+        jnp.concatenate(token_grad, axis=0),
+        down_grad[None],
+    )
+
+
+def shards(tokens, expert_ids, *rest):
+    tok_rows, top_count = expert_ids.shape
+    expert_count = lax.axis_size("expert")
+    capacity = min(tok_rows, 2 * tok_rows * top_count // expert_count)
+    body = shards_dense if capacity == tok_rows else shards_slots
+    return body(tokens, expert_ids, *rest)
 
 
 def solution(mesh):

time: 375 us -> 284 us (0.76)
  waiting for transfers between devices: 261 us -> 136 us
  blocking collectives: 0 us -> 16 us
  matrix products: 65.6 us -> 76.3 us
  other arithmetic: 8.2 us -> 12 us
    all_to_all x4, waiting for transfers between devices: 125 us -> 34.5 us  [scatter_sum(): lax.all_to_all(rows.reshape(lax.axis_size('expert'), -1, rows.shape[1]),...]
    reduce_scatter x1 -> x0, waiting for transfers between devices: 59.6 us -> none  [shards(): lax.psum_scatter(jnp.concatenate([gate_part, up_part, back_part], axis=1)...]
    all_gather x3 -> x4, waiting for transfers between devices: 75.2 us -> 99.8 us  [gather_rows(): return lax.all_gather(block, 'expert', axis=0, tiled=True)]
    all_gather x0 -> x1, blocking collectives: none -> 16 us  [gather_rows(): return lax.all_gather(block, 'expert', axis=0, tiled=True)]
    dot_general x11 -> x13, matrix products: 65.6 us -> 76.3 us  [the longest x2 12.8 us: shards_dense(): lax.dot_general(grad_gate, gate_local, last, preferred_element_type=f32)]
    ppermute x0 -> x6, starting transfers between devices: none -> 5.53 us  [swap_pieces(): return lax.ppermute(block, 'dp', [(0, 1), (1, 0)])]
  transfers between devices with their start and end apart: 8 -> 14, of which waited for: 8 -> 7; matrix products, arithmetic and copies ran while one was open for 12% -> 31% of each run, Pallas kernels for 0% -> 0%
where the time goes in v1:
time: 284 us; the launch traced here: 283 us
  waiting for transfers between devices  136 us (48%)
  matrix products  76.3 us (27%)
  starting transfers between devices  25.9 us (9%)
  blocking collectives  16 us (6%)
  between operations  14 us (5%)
  other arithmetic  12 us (4%)
  local copies, waits for them, and re-layouts  3.58 us (1%)
    all_gather x4, waiting for transfers between devices, gather_rows(): return lax.all_gather(block, 'expert', axis=0, tiled=True)  99.8 us
    all_to_all x4, waiting for transfers between devices, scatter_sum(): lax.all_to_all(rows.reshape(lax.axis_size('expert'), -1, rows.shape[1]),...  34.5 us
    all_to_all x4, starting transfers between devices, scatter_sum(): lax.all_to_all(rows.reshape(lax.axis_size('expert'), -1, rows.shape[1]),...  20.2 us
    all_gather x1, blocking collectives, gather_rows(): return lax.all_gather(block, 'expert', axis=0, tiled=True)  16 us
    dot_general x2, matrix products, shards_dense(): lax.dot_general(grad_gate, gate_local, last, preferred_element_type=f32)  12.8 us
    dot_general x2, matrix products, shards_dense(): out = jnp.dot(hidden, down_local, preferred_element_type=f32)  11.7 us
    dot_general x2, matrix products, shards_dense(): lax.dot_general(grad_up, up_local, last, preferred_element_type=f32)  11.5 us
    dot_general x2, matrix products, shards_dense(): lax.dot_general(rows_dy, down_local, last, preferred_element_type=f32)  11.2 us
  transfers between devices with their start and end apart: 14, of which 7 were waited for; matrix products, arithmetic and copies ran while one was open for 31% of the time, Pallas kernels for 0%

profile of v1, /device:TPU:11, one launch (start us, length us, event | category | flops | bytes accessed | tf_op | source)
XLA Modules:
  0.0 283.3 jit_solution(7629491277067183374)
XLA Ops:
  7.2 1.5 fusion.85
  8.8 0.7 all-gather.6.cloned.1.call-update
  9.6 1.5 fusion.84
  11.2 0.5 all-gather.10.cloned.1.call-update
  11.7 0.7 select_reduce_fusion
  12.4 16.0 %all-gather = f32[16,32,16]{1,2,0:T(8,128)S(1)} all-gather(f32[1,32,16]{1,2,0:T(8,128)S(1)} %bitcast.74), channel_id=1, replica_groups=mesh['dp'=2,'expert'=16] {'expert'}, dimensions={0}, use_global_device_ids=true | all-gather | bytes 34816 | tf_op jit(solution)/shard_map/all_gather | solution.py:142
  28.5 0.1 reshape.31
  28.6 0.1 reshape.25
  28.9 20.0 %all-gather.8.cloned.1.call-done = bf16[256,2048]{1,0:T(8,128)(2,1)} async-done(((bf16[16,2048]{1,0:T(8,128)(2,1)}), bf16[256,2048]{1,0:T(8,128)(2,1)}) %all-gather.8.cloned.1.call-update) | async-done | bytes 1048592 | tf_op jit(solution)/shard_map/all_gather | solution.py:142
  49.0 5.0 %fusion.58 = bf16[256,1536]{1,0:T(8,128)(2,1)S(1)} fusion(bf16[256,2048]{1,0:T(8,128)(2,1)} %all-gather.8.cloned.1.call-done, bf16[1,2048,1536]{2,1,0:T(8,128)(2,1)} %param.12), kind=kOutput, calls=%fused_computation.37 | convolution fusion | flops 1611005952 | bytes 8126464 | tf_op jit(solution)/shard_map/dot_general | solution.py:180
  54.0 1.3 collective-permute-start.3
  55.3 4.6 %fusion.52 = bf16[256,1536]{1,0:T(8,128)(2,1)S(1)} fusion(bf16[256,2048]{1,0:T(8,128)(2,1)S(1)} %copy-done.9, bf16[1,2048,1536]{2,1,0:T(8,128)(2,1)} %param.11), kind=kOutput, calls=%fused_computation.35 | convolution fusion | flops 1611005952 | bytes 8126464 | tf_op jit(solution)/shard_map/dot_general | solution.py:178
  59.9 0.3 collective-permute-start.2
  60.2 28.4 %all-gather.6.cloned.1.call-done = bf16[256,2048]{1,0:T(8,128)(2,1)} async-done(((bf16[16,2048]{1,0:T(8,128)(2,1)}), bf16[256,2048]{1,0:T(8,128)(2,1)}) %all-gather.6.cloned.1.call-update) | async-done | bytes 1048592 | tf_op jit(solution)/shard_map/all_gather | solution.py:142
  88.6 5.9 %fusion.55 = bf16[256,1536]{1,0:T(8,128)(2,1)} fusion(bf16[256,2048]{1,0:T(8,128)(2,1)} %all-gather.6.cloned.1.call-done, bf16[1,2048,1536]{2,1,0:T(8,128)(2,1)} %param.12), kind=kOutput, calls=%fused_computation.36 | convolution fusion | flops 1611005952 | bytes 8126464 | tf_op jit(solution)/shard_map/dot_general | solution.py:180
  94.5 1.2 collective-permute-start.1
  95.7 5.5 %fusion.49 = bf16[256,1536]{1,0:T(8,128)(2,1)} fusion(bf16[256,2048]{1,0:T(8,128)(2,1)S(1)} %copy-done.8, bf16[1,2048,1536]{2,1,0:T(8,128)(2,1)} %param.11), kind=kOutput, calls=%fused_computation.34 | convolution fusion | flops 1611005952 | bytes 8126464 | tf_op jit(solution)/shard_map/dot_general | solution.py:178
  101.1 0.3 collective-permute-start
  101.4 26.8 %all-gather.12.cloned.1.call-done = bf16[256,2048]{1,0:T(8,128)(2,1)} async-done(((bf16[16,2048]{1,0:T(8,128)(2,1)}), bf16[256,2048]{1,0:T(8,128)(2,1)}) %all-gather.12.cloned.1.call-update) | async-done | bytes 1048592 | tf_op jit(solution)/shard_map/all_gather | solution.py:142
  128.2 1.5 multiply_convert_fusion
  129.7 2.4 multiply_convert_fusion.6
  132.1 5.8 %fusion.43 = bf16[256,2048]{1,0:T(8,128)(2,1)} fusion(bf16[256,1536]{1,0:T(8,128)(2,1)S(1)} %multiply_convert_fusion.6, bf16[1,1536,2048]{2,1,0:T(8,128)(2,1)} %param.13, f32[256]{0:T(256)S(1)} %mul.81), kind=kOutput, calls=%fused_computation.32 | convolution fusion | flops 1611661312 | bytes 8127488 | tf_op jit(solution)/shard_map/dot_general | solution.py:192
  137.9 5.3 %all-to-all-start.1 = ((bf16[16,16,2048]{2,1,0:T(8,128)(2,1)}), bf16[16,16,2048]{2,1,0:T(8,128)(2,1)S(1)}, u32[]{:S(2)}, u32[]{:S(2)}) async-start(bf16[16,16,2048]{2,1,0:T(8,128)(2,1)} %bitcast.5), calls=%async_computation.1 | async-start | bytes 2097152 | tf_op jit(solution)/shard_map/all_to_all | solution.py:146
  143.2 5.5 %fusion.64 = bf16[256,1536]{1,0:T(8,128)(2,1)} fusion(bf16[256,2048]{1,0:T(8,128)(2,1)S(1)} %multiply_convert_fusion, bf16[1,1536,2048]{2,1,0:T(8,128)(2,1)} %param.13), kind=kOutput, calls=%fused_computation.39 | convolution fusion | flops 1611005952 | bytes 8126464 | tf_op jit(solution)/shard_map/dot_general | solution.py:183
  148.7 1.2 collective-permute-start.5
  149.9 24.5 %all-gather.10.cloned.1.call-done = bf16[256,2048]{1,0:T(8,128)(2,1)} async-done(((bf16[16,2048]{1,0:T(8,128)(2,1)}), bf16[256,2048]{1,0:T(8,128)(2,1)}) %all-gather.10.cloned.1.call-update) | async-done | bytes 1048592 | tf_op jit(solution)/shard_map/all_gather | solution.py:142
  174.5 1.5 multiply_convert_fusion.1
  176.0 2.8 %multiply_convert_fusion.7 = bf16[256,1536]{1,0:T(8,128)(2,1)S(1)} fusion(bf16[256,1536]{1,0:T(8,128)(2,1)} %collective-permute-done.1, bf16[256,1536]{1,0:T(8,128)(2,1)} %fusion.55, bf16[256,1536]{1,0:T(8,128)(2,1)} %collective-permute-done, bf16[256,1536]{1,0:T(8,128)(2,1)} %fusion.49), kind=kLoop, calls=%fused_computation.59 | loop fusion | flops 4718592 | bytes 3932160 | tf_op jit(solution)/shard_map/convert_element_type | solution.py:10
  178.8 5.8 %fusion.46 = bf16[256,2048]{1,0:T(8,128)(2,1)} fusion(bf16[256,1536]{1,0:T(8,128)(2,1)S(1)} %multiply_convert_fusion.7, bf16[1,1536,2048]{2,1,0:T(8,128)(2,1)} %param.13, f32[256]{0:T(256)S(1)} %mul.76), kind=kOutput, calls=%fused_computation.33 | convolution fusion | flops 1611661312 | bytes 8127488 | tf_op jit(solution)/shard_map/dot_general | solution.py:192
  184.7 5.4 %all-to-all-start = ((bf16[16,16,2048]{2,1,0:T(8,128)(2,1)}), bf16[16,16,2048]{2,1,0:T(8,128)(2,1)S(1)}, u32[]{:S(2)}, u32[]{:S(2)}) async-start(bf16[16,16,2048]{2,1,0:T(8,128)(2,1)} %bitcast.4), calls=%async_computation | async-start | bytes 2097152 | tf_op jit(solution)/shard_map/all_to_all | solution.py:146
  190.2 5.7 %fusion.61 = bf16[256,1536]{1,0:T(8,128)(2,1)} fusion(bf16[256,2048]{1,0:T(8,128)(2,1)S(1)} %multiply_convert_fusion.1, bf16[1,1536,2048]{2,1,0:T(8,128)(2,1)} %param.13), kind=kOutput, calls=%fused_computation.38 | convolution fusion | flops 1611005952 | bytes 8126464 | tf_op jit(solution)/shard_map/dot_general | solution.py:183
  195.8 1.2 collective-permute-start.4
  197.1 6.2 %fusion.17 = f32[256,2048]{1,0:T(8,128)S(1)} fusion(bf16[1,2048,1536]{2,1,0:T(8,128)(2,1)} %param.11, bf16[256,1536]{1,0:T(8,128)(2,1)} %collective-permute-done.2, bf16[256,1536]{1,0:T(8,128)(2,1)S(1)} %copy-done.6, bf16[256,1536]{1,0:T(8,128)(2,1)} %collective-permute-done.3, bf16[256,1536]{1,0:T(8,128)(2,1)S(1)} %copy-done.4, ...), kind=kOutput, calls=%fused_computation.18 | convolution fusion | flops 1618083840 | bytes 13107200 | tf_op jit(solution)/shard_map/dot_general | solution.py:194
  203.3 4.7 %fusion.37 = bf16[256,2048]{1,0:T(8,128)(2,1)} fusion(f32[256,2048]{1,0:T(8,128)S(1)} %fusion.17, bf16[1,2048,1536]{2,1,0:T(8,128)(2,1)S(1)} %bitcast.76, bf16[256,1536]{1,0:T(8,128)(2,1)} %collective-permute-done.5, bf16[256,1536]{1,0:T(8,128)(2,1)} %fusion.64, bf16[256,1536]{1,0:T(8,128)(2,1)} %collective-permute-done.2, bf16[256,1536]{1,0:T(8,128)(2,1)S(1)} %copy-done.6), kind=kOutput, calls=%fused_computation.30 | convolution fusion | flops 1616379904 | bytes 12582912 | tf_op jit(solution)/shard_map/dot_general | solution.py:195
  208.0 7.4 %all-to-all-done = bf16[16,16,2048]{2,1,0:T(8,128)(2,1)S(1)} async-done(((bf16[16,16,2048]{2,1,0:T(8,128)(2,1)}), bf16[16,16,2048]{2,1,0:T(8,128)(2,1)S(1)}, u32[]{:S(2)}, u32[]{:S(2)}) %all-to-all-start) | async-done | bytes 1048608 | tf_op jit(solution)/shard_map/all_to_all | solution.py:146
  215.4 4.5 %all-to-all-start.3 = ((bf16[16,16,2048]{2,1,0:T(8,128)(2,1)}), bf16[16,16,2048]{2,1,0:T(8,128)(2,1)S(1)}, u32[]{:S(2)}, u32[]{:S(2)}) async-start(bf16[16,16,2048]{2,1,0:T(8,128)(2,1)} %bitcast.73), calls=%async_computation.3 | async-start | bytes 2097152 | tf_op jit(solution)/shard_map/all_to_all | solution.py:146
  220.0 6.6 %fusion.19 = f32[256,2048]{1,0:T(8,128)S(1)} fusion(bf16[1,2048,1536]{2,1,0:T(8,128)(2,1)} %param.11, bf16[256,1536]{1,0:T(8,128)(2,1)} %collective-permute-done, bf16[256,1536]{1,0:T(8,128)(2,1)} %fusion.49, bf16[256,1536]{1,0:T(8,128)(2,1)} %collective-permute-done.1, bf16[256,1536]{1,0:T(8,128)(2,1)} %fusion.55, ...), kind=kOutput, calls=%fused_computation.20 | convolution fusion | flops 1618083840 | bytes 13107200 | tf_op jit(solution)/shard_map/dot_general | solution.py:194
  226.6 6.8 %fusion.40 = bf16[256,2048]{1,0:T(8,128)(2,1)} fusion(f32[256,2048]{1,0:T(8,128)S(1)} %fusion.19, bf16[1,2048,1536]{2,1,0:T(8,128)(2,1)} %param.12, bf16[256,1536]{1,0:T(8,128)(2,1)} %collective-permute-done.4, bf16[256,1536]{1,0:T(8,128)(2,1)} %fusion.61, bf16[256,1536]{1,0:T(8,128)(2,1)} %collective-permute-done, bf16[256,1536]{1,0:T(8,128)(2,1)} %fusion.49), kind=kOutput, calls=%fused_computation.31 | convolution fusion | flops 1616379904 | bytes 12582912 | tf_op jit(solution)/shard_map/dot_general | solution.py:195
  233.4 11.4 %all-to-all-done.3 = bf16[16,16,2048]{2,1,0:T(8,128)(2,1)S(1)} async-done(((bf16[16,16,2048]{2,1,0:T(8,128)(2,1)}), bf16[16,16,2048]{2,1,0:T(8,128)(2,1)S(1)}, u32[]{:S(2)}, u32[]{:S(2)}) %all-to-all-start.3) | async-done | bytes 1048608 | tf_op jit(solution)/shard_map/all_to_all | solution.py:146
  244.8 4.9 %all-to-all-start.2 = ((bf16[16,16,2048]{2,1,0:T(8,128)(2,1)}), bf16[16,16,2048]{2,1,0:T(8,128)(2,1)}, u32[]{:S(2)}, u32[]{:S(2)}) async-start(bf16[16,16,2048]{2,1,0:T(8,128)(2,1)} %bitcast.72), calls=%async_computation.2 | async-start | bytes 2097152 | tf_op jit(solution)/shard_map/all_to_all | solution.py:146
  249.8 8.2 %fusion = bf16[1,1536,2048]{2,1,0:T(8,128)(2,1)} fusion(bf16[256,2048]{1,0:T(8,128)(2,1)} %copy-done, bf16[256,2048]{1,0:T(8,128)(2,1)} %copy-done.1, bf16[256,1536]{1,0:T(8,128)(2,1)} %copy-done.2, bf16[256,1536]{1,0:T(8,128)(2,1)} %copy-done.7), kind=kOutput, calls=%fused_computation.1 | convolution fusion | flops 3231711232 | bytes 9961472 | tf_op jit(solution)/shard_map/dot_general | solution.py:199
  258.0 0.1 reduce_sum.59
  258.1 0.1 reduce_sum.58
  258.3 0.1 reduce_sum.61
  258.4 0.7 pad_maximum_fusion
  259.1 15.7 %all-to-all-done.2 = bf16[16,16,2048]{2,1,0:T(8,128)(2,1)} async-done(((bf16[16,16,2048]{2,1,0:T(8,128)(2,1)}), bf16[16,16,2048]{2,1,0:T(8,128)(2,1)}, u32[]{:S(2)}, u32[]{:S(2)}) %all-to-all-start.2) | async-done | bytes 1048608 | tf_op jit(solution)/shard_map/all_to_all | solution.py:146
  274.7 1.4 reduce_sum.60
  276.1 0.7 pad_maximum_fusion.1
  (43 shorter events, 0.5 us)
Async XLA Ops:
  7.2 41.8 %all-gather.8.cloned.1.call-start = ((), (), s32[]{:S(2)}) async-start(), calls=%async_computation.5 | async-start | bytes 1114112 | tf_op jit(solution)/shard_map/all_gather | solution.py:142
  8.8 79.8 %all-gather.6.cloned.1.call-start = ((), (), s32[]{:S(2)}) async-start(), calls=%async_computation.4 | async-start | bytes 1114112 | tf_op jit(solution)/shard_map/all_gather | solution.py:142
  9.5 118.7 %all-gather.12.cloned.1.call-start = ((), (), s32[]{:S(2)}) async-start(), calls=%async_computation.7 | async-start | bytes 1114112 | tf_op jit(solution)/shard_map/all_gather | solution.py:142
  11.1 163.4 %all-gather.10.cloned.1.call-start = ((), (), s32[]{:S(2)}) async-start(), calls=%async_computation.6 | async-start | bytes 1114112 | tf_op jit(solution)/shard_map/all_gather | solution.py:142
  49.0 6.3 %copy-start.9 = (bf16[256,2048]{1,0:T(8,128)(2,1)S(1)}, bf16[256,2048]{1,0:T(8,128)(2,1)}, u32[]{:S(2)}) copy-start(bf16[256,2048]{1,0:T(8,128)(2,1)} %all-gather.8.cloned.1.call-done) | copy-start | bytes 3145732
  54.0 75.7 %copy-start.3 = (bf16[256,1536]{1,0:T(8,128)(2,1)}, bf16[256,1536]{1,0:T(8,128)(2,1)S(1)}, u32[]{:S(2)}) copy-start(bf16[256,1536]{1,0:T(8,128)(2,1)S(1)} %fusion.58) | copy-start | bytes 2359300
  54.0 75.7 %collective-permute-start.3 = (bf16[256,1536]{1,0:T(8,128)(2,1)S(1)}, bf16[256,1536]{1,0:T(8,128)(2,1)}, u32[]{:S(2)}, u32[]{:S(2)}) collective-permute-start(bf16[256,1536]{1,0:T(8,128)(2,1)S(1)} %fusion.58), channel_id=1, source_target_pairs={{0,16},{16,0},{1,17},{17,1},{2,18},{18,2},{3,19},{19,3},{4,20},{20... | collective-permute-start | bytes 2359304 | tf_op jit(solution)/shard_map/ppermute | solution.py:153
  59.9 69.8 %copy-start.5 = (bf16[256,1536]{1,0:T(8,128)(2,1)}, bf16[256,1536]{1,0:T(8,128)(2,1)S(1)}, u32[]{:S(2)}) copy-start(bf16[256,1536]{1,0:T(8,128)(2,1)S(1)} %fusion.52) | copy-start | bytes 2359300
  59.9 69.8 %collective-permute-start.2 = (bf16[256,1536]{1,0:T(8,128)(2,1)S(1)}, bf16[256,1536]{1,0:T(8,128)(2,1)}, u32[]{:S(2)}, u32[]{:S(2)}) collective-permute-start(bf16[256,1536]{1,0:T(8,128)(2,1)S(1)} %fusion.52), channel_id=1, source_target_pairs={{0,16},{16,0},{1,17},{17,1},{2,18},{18,2},{3,19},{19,3},{4,20},{20... | collective-permute-start | bytes 2359304 | tf_op jit(solution)/shard_map/ppermute | solution.py:153
  88.6 7.1 %copy-start.8 = (bf16[256,2048]{1,0:T(8,128)(2,1)S(1)}, bf16[256,2048]{1,0:T(8,128)(2,1)}, u32[]{:S(2)}) copy-start(bf16[256,2048]{1,0:T(8,128)(2,1)} %all-gather.6.cloned.1.call-done) | copy-start | bytes 3145732
  94.5 81.5 %collective-permute-start.1 = (bf16[256,1536]{1,0:T(8,128)(2,1)}, bf16[256,1536]{1,0:T(8,128)(2,1)}, u32[]{:S(2)}, u32[]{:S(2)}) collective-permute-start(bf16[256,1536]{1,0:T(8,128)(2,1)} %fusion.55), channel_id=1, source_target_pairs={{0,16},{16,0},{1,17},{17,1},{2,18},{18,2},{3,19},{19,3},{4,20},{20... | collective-permute-start | bytes 2359304 | tf_op jit(solution)/shard_map/ppermute | solution.py:153
  101.1 74.8 %collective-permute-start = (bf16[256,1536]{1,0:T(8,128)(2,1)}, bf16[256,1536]{1,0:T(8,128)(2,1)}, u32[]{:S(2)}, u32[]{:S(2)}) collective-permute-start(bf16[256,1536]{1,0:T(8,128)(2,1)} %fusion.49), channel_id=1, source_target_pairs={{0,16},{16,0},{1,17},{17,1},{2,18},{18,2},{3,19},{19,3},{4,20},{20... | collective-permute-start | bytes 2359304 | tf_op jit(solution)/shard_map/ppermute | solution.py:153
  129.7 13.5 %copy-start = (bf16[256,2048]{1,0:T(8,128)(2,1)}, bf16[256,2048]{1,0:T(8,128)(2,1)S(1)}, u32[]{:S(2)}) copy-start(bf16[256,2048]{1,0:T(8,128)(2,1)S(1)} %multiply_convert_fusion) | copy-start | bytes 3145732
  132.1 5.8 %copy-start.2 = (bf16[256,1536]{1,0:T(8,128)(2,1)}, bf16[256,1536]{1,0:T(8,128)(2,1)S(1)}, u32[]{:S(2)}) copy-start(bf16[256,1536]{1,0:T(8,128)(2,1)S(1)} %multiply_convert_fusion.6) | copy-start | bytes 2359300
  137.9 46.8 %all-to-all-start.1 = ((bf16[16,16,2048]{2,1,0:T(8,128)(2,1)}), bf16[16,16,2048]{2,1,0:T(8,128)(2,1)S(1)}, u32[]{:S(2)}, u32[]{:S(2)}) async-start(bf16[16,16,2048]{2,1,0:T(8,128)(2,1)} %bitcast.5), calls=%async_computation.1 | async-start | bytes 2097152 | tf_op jit(solution)/shard_map/all_to_all | solution.py:146
  148.7 48.3 %collective-permute-start.5 = (bf16[256,1536]{1,0:T(8,128)(2,1)}, bf16[256,1536]{1,0:T(8,128)(2,1)}, u32[]{:S(2)}, u32[]{:S(2)}) collective-permute-start(bf16[256,1536]{1,0:T(8,128)(2,1)} %fusion.64), channel_id=1, source_target_pairs={{0,16},{16,0},{1,17},{17,1},{2,18},{18,2},{3,19},{19,3},{4,20},{20... | collective-permute-start | bytes 2359304 | tf_op jit(solution)/shard_map/ppermute | solution.py:153
  176.0 14.2 %copy-start.1 = (bf16[256,2048]{1,0:T(8,128)(2,1)}, bf16[256,2048]{1,0:T(8,128)(2,1)S(1)}, u32[]{:S(2)}) copy-start(bf16[256,2048]{1,0:T(8,128)(2,1)S(1)} %multiply_convert_fusion.1) | copy-start | bytes 3145732
  178.8 5.9 %copy-start.7 = (bf16[256,1536]{1,0:T(8,128)(2,1)}, bf16[256,1536]{1,0:T(8,128)(2,1)S(1)}, u32[]{:S(2)}) copy-start(bf16[256,1536]{1,0:T(8,128)(2,1)S(1)} %multiply_convert_fusion.7) | copy-start | bytes 2359300
  184.7 30.7 %all-to-all-start = ((bf16[16,16,2048]{2,1,0:T(8,128)(2,1)}), bf16[16,16,2048]{2,1,0:T(8,128)(2,1)S(1)}, u32[]{:S(2)}, u32[]{:S(2)}) async-start(bf16[16,16,2048]{2,1,0:T(8,128)(2,1)} %bitcast.4), calls=%async_computation | async-start | bytes 2097152 | tf_op jit(solution)/shard_map/all_to_all | solution.py:146
  190.1 7.0 %copy-start.4 = (bf16[256,1536]{1,0:T(8,128)(2,1)S(1)}, bf16[256,1536]{1,0:T(8,128)(2,1)}, u32[]{:S(2)}) copy-start(bf16[256,1536]{1,0:T(8,128)(2,1)} %copy-done.3) | copy-start | bytes 2359300
  190.1 6.9 %copy-start.6 = (bf16[256,1536]{1,0:T(8,128)(2,1)S(1)}, bf16[256,1536]{1,0:T(8,128)(2,1)}, u32[]{:S(2)}) copy-start(bf16[256,1536]{1,0:T(8,128)(2,1)} %copy-done.5) | copy-start | bytes 2359300
  190.2 13.1 %slice-start = ((s8[6291456]{0:T(1024)(128)(4,1)}), s8[4194304]{0:T(1024)(128)(4,1)S(1)}, s32[]{:S(2)}) async-start(s8[6291456]{0:T(1024)(128)(4,1)} %bitcast.75), calls=%async_computation.8 | async-start | bytes 8388608
  195.8 7.5 %slice-start.1 = ((s8[6291456]{0:T(1024)(128)(4,1)}), s8[2097152]{0:T(1024)(128)(4,1)S(1)}, s32[]{:S(2)}) async-start(s8[6291456]{0:T(1024)(128)(4,1)} %bitcast.75), calls=%async_computation.9 | async-start | bytes 4194304
  195.8 24.1 %collective-permute-start.4 = (bf16[256,1536]{1,0:T(8,128)(2,1)}, bf16[256,1536]{1,0:T(8,128)(2,1)}, u32[]{:S(2)}, u32[]{:S(2)}) collective-permute-start(bf16[256,1536]{1,0:T(8,128)(2,1)} %fusion.61), channel_id=1, source_target_pairs={{0,16},{16,0},{1,17},{17,1},{2,18},{18,2},{3,19},{19,3},{4,20},{20... | collective-permute-start | bytes 2359304 | tf_op jit(solution)/shard_map/ppermute | solution.py:153
  215.4 29.4 %all-to-all-start.3 = ((bf16[16,16,2048]{2,1,0:T(8,128)(2,1)}), bf16[16,16,2048]{2,1,0:T(8,128)(2,1)S(1)}, u32[]{:S(2)}, u32[]{:S(2)}) async-start(bf16[16,16,2048]{2,1,0:T(8,128)(2,1)} %bitcast.73), calls=%async_computation.3 | async-start | bytes 2097152 | tf_op jit(solution)/shard_map/all_to_all | solution.py:146
  244.8 29.9 %all-to-all-start.2 = ((bf16[16,16,2048]{2,1,0:T(8,128)(2,1)}), bf16[16,16,2048]{2,1,0:T(8,128)(2,1)}, u32[]{:S(2)}, u32[]{:S(2)}) async-start(bf16[16,16,2048]{2,1,0:T(8,128)(2,1)} %bitcast.72), calls=%async_computation.2 | async-start | bytes 2097152 | tf_op jit(solution)/shard_map/all_to_all | solution.py:146
Sparse Core Ops, SparseCore 0:
  10.7 38.2 all-gather.7
  51.7 36.8 all-gather.5
  91.3 36.8 all-gather.11
  130.2 44.2 all-gather.9

commit v2 on v1

--- a/solution.py
+++ b/solution.py
@@ -1,6 +1,10 @@
+import functools
+
 import jax
 import jax.numpy as jnp
 from jax import lax
+from jax.experimental import pallas as pl
+from jax.experimental.pallas import tpu as pltpu
 from jax.sharding import PartitionSpec as P
 
 
@@ -138,8 +142,91 @@
 CHUNKS = 2
 
 
-def gather_rows(block):
-    return lax.all_gather(block, "expert", axis=0, tiled=True)
+def gather_kernel(depth, count, *refs):
+    ins, outs = refs[:count], refs[count : 2 * count]
+    send_sem, recv_sem, own_sem = refs[2 * count :]
+    me, piece = lax.axis_index("expert"), lax.axis_index("dp")
+    z, x, core = me // 4, (me // 2) % 2, me % 2
+
+    def place(z_at, x_at, core_at):
+        return (z_at * 2 + x_at) * 2 + core_at
+
+    across, sibling = place(z, 1 - x, core), place(z, x, 1 - core)
+    along = [place(lax.rem(z + k, depth), x, core) for k in range(1, depth)]
+    barrier = pltpu.get_barrier_semaphore()
+    for peer in [*along, across, sibling]:
+        pl.semaphore_signal(
+            barrier, inc=1, device_id=(piece, peer), device_id_type=pl.DeviceIdType.MESH
+        )
+    pl.semaphore_wait(barrier, depth + 1)
+
+    def copy(a, src, slot, sem, peer):
+        return pltpu.make_async_remote_copy(
+            src_ref=src,
+            dst_ref=outs[a].at[slot],
+            send_sem=send_sem.at[a, sem],
+            recv_sem=recv_sem.at[a, sem],
+            device_id=(piece, peer),
+            device_id_type=pl.DeviceIdType.MESH,
+        )
+
+    own, started = [], []
+    x_step = {}
+    core_step = {}
+    z_step = {}
+    for a in range(count):
+        own.append(pltpu.make_async_copy(ins[a], outs[a].at[me], own_sem.at[a]))
+        own[-1].start()
+        for k in range(1, depth):
+            z_step[a, k] = copy(a, ins[a], me, k - 1, along[k - 1])
+            z_step[a, k].start()
+        x_step[a, 0] = copy(a, ins[a], me, depth - 1, across)
+        x_step[a, 0].start()
+        core_step[a, 0] = copy(a, ins[a], me, 2 * depth - 1, sibling)
+        core_step[a, 0].start()
+    for k in range(1, depth):
+        for a in range(count):
+            z_step[a, k].wait_recv()
+            slot = place(lax.rem(z + depth - k, depth), x, core)
+            x_step[a, k] = copy(a, outs[a].at[slot], slot, depth - 1 + k, across)
+            x_step[a, k].start()
+            core_step[a, k] = copy(a, outs[a].at[slot], slot, 2 * depth - 1 + k, sibling)
+            core_step[a, k].start()
+    for k in range(depth):
+        for a in range(count):
+            x_step[a, k].wait_recv()
+            slot = place(lax.rem(z + depth - k, depth), 1 - x, core)
+            core_step[a, depth + k] = copy(
+                a, outs[a].at[slot], slot, 3 * depth - 1 + k, sibling
+            )
+            core_step[a, depth + k].start()
+    for a in range(count):
+        for k in range(2 * depth):
+            core_step[a, k].wait_recv()
+        own[a].wait()
+        for step in (z_step, x_step, core_step):
+            for key, made in step.items():
+                if key[0] == a:
+                    made.wait_send()
+
+
+def gather_rows(number, *blocks):
+    experts = lax.axis_size("expert")
+    depth, count = experts // 4, len(blocks)
+    moved = sum(experts * b.size * b.dtype.itemsize for b in blocks)
+    return pl.pallas_call(
+        functools.partial(gather_kernel, depth, count),
+        out_shape=[jax.ShapeDtypeStruct((experts, *b.shape), b.dtype) for b in blocks],
+        in_specs=[pl.BlockSpec(memory_space=pl.ANY)] * count,
+        out_specs=[pl.BlockSpec(memory_space=pl.ANY)] * count,
+        scratch_shapes=[
+            pltpu.SemaphoreType.DMA((count, 4 * depth - 1)),
+            pltpu.SemaphoreType.DMA((count, 4 * depth - 1)),
+            pltpu.SemaphoreType.DMA((count,)),
+        ],
+        compiler_params=pltpu.CompilerParams(collective_id=number, has_side_effects=True),
+        cost_estimate=pl.CostEstimate(flops=0, bytes_accessed=16 * moved, transcendentals=0),
+    )(*blocks)
 
 
 def scatter_sum(rows):
@@ -161,21 +248,29 @@
     me = lax.axis_index("expert")
     named = expert_ids[:, :, None] == jnp.arange(expert_count, dtype=jnp.int32)[None, None, :]
     dense = jnp.sum(jnp.where(named, route_weights[:, :, None], 0.0), axis=1)
-    all_weights = gather_rows(dense)
-    mine = lax.dynamic_slice_in_dim(all_weights, me, 1, axis=1).reshape(
-        expert_count, chunks, step
-    )
+    lanes = jnp.pad(dense, ((0, 0), (0, 128 - expert_count)))
+    all_x, all_weights = gather_rows(0, tokens, lanes)
+    mine = lax.dynamic_slice_in_dim(all_weights, me, 1, axis=2)
     gate_local, up_local, down_local = w_gate[0], w_up[0], w_down[0]
     last = (((1,), (1,)), ((), ()))
     first = (((0,), (0,)), ((), ()))
     f32 = jnp.float32
-    xs = [gather_rows(tokens[c * step : (c + 1) * step]) for c in range(chunks)]
-    cs = [gather_rows(cotangent[c * step : (c + 1) * step]) for c in range(chunks)]
-    ws = [mine[:, c, :].reshape(expert_count * step, 1) for c in range(chunks)]
+
+    def part(whole, c):
+        return whole[:, c * step : (c + 1) * step].reshape(expert_count * step, -1)
+
+    xs = [part(all_x, c) for c in range(chunks)]
+    ws = [part(mine, c) for c in range(chunks)]
+    gate_parts = [
+        jnp.dot(x, gate_local, preferred_element_type=f32).astype(jnp.bfloat16) for x in xs
+    ]
+    cotangent, *gate_parts = lax.optimization_barrier((cotangent, *gate_parts))
+    (all_dy,) = gather_rows(1, cotangent)
+    cs = [part(all_dy, c) for c in range(chunks)]
     hiddens, dys, mixed, token_grad = [], [], [], []
     for c in range(chunks):
         rows_x = xs[c]
-        gate_part = jnp.dot(rows_x, gate_local, preferred_element_type=f32).astype(jnp.bfloat16)
+        gate_part = gate_parts[c]
         gate_other = swap_pieces(gate_part)
         up_part = jnp.dot(rows_x, up_local, preferred_element_type=f32).astype(jnp.bfloat16)
         up_other = swap_pieces(up_part)

time: 284 us -> 210 us (0.74)
  waiting for transfers between devices: 136 us -> 45.4 us
  Pallas kernels: 0 us -> 49.2 us
  blocking collectives: 16 us -> 0 us
  between operations: 14 us -> 0.96 us
  matrix products: 76.3 us -> 63.7 us
  starting transfers between devices: 25.9 us -> 33.8 us
    all_gather x4 -> x0, waiting for transfers between devices: 99.8 us -> none  [gather_rows(): return lax.all_gather(block, 'expert', axis=0, tiled=True)]
    pallas_call x0 -> x2, Pallas kernels: none -> 49.2 us  [gather_rows(): pl.pallas_call(functools.partial(gather_kernel, depth, count), out_shape=...]
    all_gather x1 -> x0, blocking collectives: 16 us -> none  [gather_rows(): return lax.all_gather(block, 'expert', axis=0, tiled=True)]
    ppermute x6, waiting for transfers between devices: 0.02 us -> 11.9 us  [swap_pieces(): return lax.ppermute(block, 'dp', [(0, 1), (1, 0)])]
    all_to_all x4, starting transfers between devices: 20.2 us -> 28.3 us  [scatter_sum(): lax.all_to_all(rows.reshape(lax.axis_size('expert'), -1, rows.shape[1]),...]
    dot_general x2, matrix products: 10.8 us -> 4.46 us  [shards_dense(): jnp.dot(rows_x, up_local, preferred_element_type=f32).astype(jnp.bfloat16)]
    dot_general x1, matrix products: 8.19 us -> 5.34 us  [shards_dense(): lax.dot_general(jnp.concatenate(hiddens, axis=0), jnp.concatenate(dys, ax...]
  transfers between devices with their start and end apart: 14 -> 10, of which waited for: 7 -> 5; matrix products, arithmetic and copies ran while one was open for 31% -> 31% of each run, Pallas kernels for 0% -> 12%
where the time goes in v2:
time: 210 us
  matrix products  63.7 us (30%)
  Pallas kernels  49.2 us (23%)
  waiting for transfers between devices  45.4 us (22%)
  starting transfers between devices  33.8 us (16%)
  other arithmetic  11.6 us (6%)
  local copies, waits for them, and re-layouts  5.17 us (2%)
    pallas_call x2, Pallas kernels, gather_rows(): pl.pallas_call(functools.partial(gather_kernel, depth, count), out_shape=...  49.2 us
    all_to_all x4, waiting for transfers between devices, scatter_sum(): lax.all_to_all(rows.reshape(lax.axis_size('expert'), -1, rows.shape[1]),...  33.5 us
    all_to_all x4, starting transfers between devices, scatter_sum(): lax.all_to_all(rows.reshape(lax.axis_size('expert'), -1, rows.shape[1]),...  28.3 us
    dot_general x2, matrix products, shards_dense(): lax.dot_general(grad_gate, gate_local, last, preferred_element_type=f32)  12.3 us
    ppermute x6, waiting for transfers between devices, swap_pieces(): return lax.ppermute(block, 'dp', [(0, 1), (1, 0)])  11.9 us
    dot_general x2, matrix products, shards_dense(): lax.dot_general(rows_dy, down_local, last, preferred_element_type=f32)  11.5 us
    dot_general x2, matrix products, shards_dense(): out = jnp.dot(hidden, down_local, preferred_element_type=f32)  11.4 us
    dot_general x2, matrix products, shards_dense(): lax.dot_general(grad_up, up_local, last, preferred_element_type=f32)  11.3 us
  transfers between devices with their start and end apart: 10, of which 5 were waited for; matrix products, arithmetic and copies ran while one was open for 31% of the time, Pallas kernels for 12%

profile of v2, /device:TPU:11, one launch (start us, length us, event | category | flops | bytes accessed | tf_op | source)
XLA Modules:
  0.0 209.7 jit_solution(3162074551520478794)
XLA Ops:
  0.6 0.7 select_reduce_fusion
  1.4 0.6 pad.4.refs_1_
  2.0 23.5 %shard_map.94 = (bf16[16,32,2048]{2,1,0:T(8,128)(2,1)}, f32[16,32,128]{2,1,0:T(8,128)}) custom-call(bf16[32,2048]{1,0:T(8,128)(2,1)} %refs_0_.1, f32[32,128]{1,0:T(8,128)} %pad.4.refs_1_), custom_call_target="tpu_custom_call" | custom-call | bytes 37748736 | tf_op jit(solution)/shard_map/pallas_call | solution.py:217
  25.6 1.8 fusion.86
  27.5 4.7 %fusion.52 = bf16[256,1536]{1,0:T(8,128)(2,1)S(1)} fusion(bf16[256,2048]{1,0:T(8,128)(2,1)S(1)} %bitcast.88, bf16[1,2048,1536]{2,1,0:T(8,128)(2,1)} %param.11), kind=kOutput, calls=%fused_computation.35 | convolution fusion | flops 1611005952 | bytes 8126464 | tf_op jit(solution)/shard_map/dot_general | solution.py:265
  32.2 2.7 %fusion.49 = bf16[256,1536]{1,0:T(8,128)(2,1)} fusion(bf16[256,2048]{1,0:T(8,128)(2,1)S(1)} %bitcast.86, bf16[1,2048,1536]{2,1,0:T(8,128)(2,1)S(1)} %bitcast.92), kind=kOutput, calls=%fused_computation.34 | convolution fusion | flops 1611005952 | bytes 8126464 | tf_op jit(solution)/shard_map/dot_general | solution.py:265
  34.9 1.2 collective-permute-start.2
  36.2 1.8 fusion.58
  38.0 0.3 collective-permute-start.3
  38.3 1.2 collective-permute-start
  39.5 2.7 %fusion.55 = bf16[256,1536]{1,0:T(8,128)(2,1)} fusion(bf16[256,2048]{1,0:T(8,128)(2,1)S(1)} %bitcast.87, bf16[1,2048,1536]{2,1,0:T(8,128)(2,1)S(1)} %bitcast.94), kind=kOutput, calls=%fused_computation.36 | convolution fusion | flops 1611005952 | bytes 8126464 | tf_op jit(solution)/shard_map/dot_general | solution.py:275
  42.2 0.2 collective-permute-start.1
  42.4 0.2 dynamic-slice_reduce_fusion.1
  42.8 25.6 %shard_map.95 = bf16[16,32,2048]{2,1,0:T(8,128)(2,1)} custom-call(bf16[32,2048]{1,0:T(8,128)(2,1)} %refs_0_.2), custom_call_target="tpu_custom_call" | custom-call | bytes 33554432 | tf_op jit(solution)/shard_map/pallas_call | solution.py:217
  68.4 2.4 %collective-permute-done.3 = bf16[256,1536]{1,0:T(8,128)(2,1)S(1)} collective-permute-done((bf16[256,1536]{1,0:T(8,128)(2,1)S(1)}, bf16[256,1536]{1,0:T(8,128)(2,1)S(1)}, u32[]{:S(2)}, u32[]{:S(2)}) %collective-permute-start.3) | collective-permute-done | bytes 786464 | tf_op jit(solution)/shard_map/ppermute | solution.py:240
  70.8 0.6 multiply_convert_fusion.6
  71.5 0.2 copy-done.9
  71.7 5.8 %fusion.43 = bf16[256,2048]{1,0:T(8,128)(2,1)} fusion(bf16[256,1536]{1,0:T(8,128)(2,1)S(1)} %multiply_convert_fusion.6, bf16[1,1536,2048]{2,1,0:T(8,128)(2,1)} %param.13, f32[256]{0:T(256)S(1)} %mul.95), kind=kOutput, calls=%fused_computation.32 | convolution fusion | flops 1611661312 | bytes 8127488 | tf_op jit(solution)/shard_map/dot_general | solution.py:287
  77.5 9.4 %all-to-all-start.1 = ((bf16[16,16,2048]{2,1,0:T(8,128)(2,1)}), bf16[16,16,2048]{2,1,0:T(8,128)(2,1)S(1)}, u32[]{:S(2)}, u32[]{:S(2)}) async-start(bf16[16,16,2048]{2,1,0:T(8,128)(2,1)} %bitcast.84), calls=%async_computation.1 | async-start | bytes 2097152 | tf_op jit(solution)/shard_map/all_to_all | solution.py:233
  87.0 1.3 multiply_convert_fusion.1
  88.3 5.6 %fusion.64 = bf16[256,1536]{1,0:T(8,128)(2,1)} fusion(bf16[256,2048]{1,0:T(8,128)(2,1)S(1)} %bitcast.90, bf16[1,1536,2048]{2,1,0:T(8,128)(2,1)} %param.13), kind=kOutput, calls=%fused_computation.39 | convolution fusion | flops 1611005952 | bytes 8126464 | tf_op jit(solution)/shard_map/dot_general | solution.py:278
  93.8 1.2 collective-permute-start.5
  95.1 9.5 %collective-permute-done.1 = bf16[256,1536]{1,0:T(8,128)(2,1)} collective-permute-done((bf16[256,1536]{1,0:T(8,128)(2,1)}, bf16[256,1536]{1,0:T(8,128)(2,1)}, u32[]{:S(2)}, u32[]{:S(2)}) %collective-permute-start.1) | collective-permute-done | bytes 786464 | tf_op jit(solution)/shard_map/ppermute | solution.py:240
  104.6 2.5 %multiply_convert_fusion.7 = bf16[256,1536]{1,0:T(8,128)(2,1)S(1)} fusion(bf16[256,1536]{1,0:T(8,128)(2,1)} %collective-permute-done.1, bf16[256,1536]{1,0:T(8,128)(2,1)} %fusion.55, bf16[256,1536]{1,0:T(8,128)(2,1)} %collective-permute-done, bf16[256,1536]{1,0:T(8,128)(2,1)} %fusion.49), kind=kLoop, calls=%fused_computation.63 | loop fusion | flops 4718592 | bytes 3932160 | tf_op jit(solution)/shard_map/convert_element_type | solution.py:14
  107.1 0.9 copy-done.11
  108.0 5.5 %fusion.46 = bf16[256,2048]{1,0:T(8,128)(2,1)} fusion(bf16[256,1536]{1,0:T(8,128)(2,1)S(1)} %multiply_convert_fusion.7, bf16[1,1536,2048]{2,1,0:T(8,128)(2,1)} %param.13, f32[256]{0:T(256)S(1)} %mul.90), kind=kOutput, calls=%fused_computation.33 | convolution fusion | flops 1611661312 | bytes 8127488 | tf_op jit(solution)/shard_map/dot_general | solution.py:287
  113.5 9.3 %all-to-all-start = ((bf16[16,16,2048]{2,1,0:T(8,128)(2,1)}), bf16[16,16,2048]{2,1,0:T(8,128)(2,1)}, u32[]{:S(2)}, u32[]{:S(2)}) async-start(bf16[16,16,2048]{2,1,0:T(8,128)(2,1)} %bitcast.82), calls=%async_computation | async-start | bytes 2097152 | tf_op jit(solution)/shard_map/all_to_all | solution.py:233
  122.9 6.0 %fusion.61 = bf16[256,1536]{1,0:T(8,128)(2,1)} fusion(bf16[256,2048]{1,0:T(8,128)(2,1)} %bitcast.85, bf16[1,1536,2048]{2,1,0:T(8,128)(2,1)} %param.13), kind=kOutput, calls=%fused_computation.38 | convolution fusion | flops 1611005952 | bytes 8126464 | tf_op jit(solution)/shard_map/dot_general | solution.py:278
  128.8 1.2 collective-permute-start.4
  130.1 5.7 %fusion.17 = f32[256,2048]{1,0:T(8,128)S(1)} fusion(bf16[1,2048,1536]{2,1,0:T(8,128)(2,1)} %param.11, bf16[256,1536]{1,0:T(8,128)(2,1)S(1)} %copy-done.6, bf16[256,1536]{1,0:T(8,128)(2,1)S(1)} %copy-done.2, bf16[256,1536]{1,0:T(8,128)(2,1)S(1)} %copy-done.10, bf16[256,1536]{1,0:T(8,128)(2,1)S(1)} %copy-done.8, ...), kind=kOutput, calls=%fused_computation.18 | convolution fusion | flops 1618083840 | bytes 13107200 | tf_op jit(solution)/shard_map/dot_general | solution.py:289
  135.8 4.5 %fusion.37 = bf16[256,2048]{1,0:T(8,128)(2,1)} fusion(f32[256,2048]{1,0:T(8,128)S(1)} %fusion.17, bf16[1,2048,1536]{2,1,0:T(8,128)(2,1)S(1)} %bitcast.96, bf16[256,1536]{1,0:T(8,128)(2,1)} %collective-permute-done.5, bf16[256,1536]{1,0:T(8,128)(2,1)} %fusion.64, bf16[256,1536]{1,0:T(8,128)(2,1)S(1)} %copy-done.6, bf16[256,1536]{1,0:T(8,128)(2,1)S(1)} %copy-done.2), kind=kOutput, calls=%fused_computation.30 | convolution fusion | flops 1616379904 | bytes 12582912 | tf_op jit(solution)/shard_map/dot_general | solution.py:290
  140.3 7.8 %all-to-all-done = bf16[16,16,2048]{2,1,0:T(8,128)(2,1)} async-done(((bf16[16,16,2048]{2,1,0:T(8,128)(2,1)}), bf16[16,16,2048]{2,1,0:T(8,128)(2,1)}, u32[]{:S(2)}, u32[]{:S(2)}) %all-to-all-start) | async-done | bytes 1048608 | tf_op jit(solution)/shard_map/all_to_all | solution.py:233
  148.1 4.6 %all-to-all-start.3 = ((bf16[16,16,2048]{2,1,0:T(8,128)(2,1)}), bf16[16,16,2048]{2,1,0:T(8,128)(2,1)}, u32[]{:S(2)}, u32[]{:S(2)}) async-start(bf16[16,16,2048]{2,1,0:T(8,128)(2,1)} %bitcast.83), calls=%async_computation.3 | async-start | bytes 2097152 | tf_op jit(solution)/shard_map/all_to_all | solution.py:233
  152.7 6.6 %fusion.19 = f32[256,2048]{1,0:T(8,128)S(1)} fusion(bf16[1,2048,1536]{2,1,0:T(8,128)(2,1)} %param.11, bf16[256,1536]{1,0:T(8,128)(2,1)} %collective-permute-done, bf16[256,1536]{1,0:T(8,128)(2,1)} %fusion.49, bf16[256,1536]{1,0:T(8,128)(2,1)} %collective-permute-done.1, bf16[256,1536]{1,0:T(8,128)(2,1)} %fusion.55, ...), kind=kOutput, calls=%fused_computation.20 | convolution fusion | flops 1618083840 | bytes 13107200 | tf_op jit(solution)/shard_map/dot_general | solution.py:289
  159.4 6.8 %fusion.40 = bf16[256,2048]{1,0:T(8,128)(2,1)} fusion(f32[256,2048]{1,0:T(8,128)S(1)} %fusion.19, bf16[1,2048,1536]{2,1,0:T(8,128)(2,1)} %param.12, bf16[256,1536]{1,0:T(8,128)(2,1)} %collective-permute-done.4, bf16[256,1536]{1,0:T(8,128)(2,1)} %fusion.61, bf16[256,1536]{1,0:T(8,128)(2,1)} %collective-permute-done, bf16[256,1536]{1,0:T(8,128)(2,1)} %fusion.49), kind=kOutput, calls=%fused_computation.31 | convolution fusion | flops 1616379904 | bytes 12582912 | tf_op jit(solution)/shard_map/dot_general | solution.py:290
  166.2 11.5 %all-to-all-done.3 = bf16[16,16,2048]{2,1,0:T(8,128)(2,1)} async-done(((bf16[16,16,2048]{2,1,0:T(8,128)(2,1)}), bf16[16,16,2048]{2,1,0:T(8,128)(2,1)}, u32[]{:S(2)}, u32[]{:S(2)}) %all-to-all-start.3) | async-done | bytes 1048608 | tf_op jit(solution)/shard_map/all_to_all | solution.py:233
  177.7 4.9 %all-to-all-start.2 = ((bf16[16,16,2048]{2,1,0:T(8,128)(2,1)}), bf16[16,16,2048]{2,1,0:T(8,128)(2,1)}, u32[]{:S(2)}, u32[]{:S(2)}) async-start(bf16[16,16,2048]{2,1,0:T(8,128)(2,1)} %bitcast.81), calls=%async_computation.2 | async-start | bytes 2097152 | tf_op jit(solution)/shard_map/all_to_all | solution.py:233
  182.6 0.5 slice_convert_fusion.1
  183.2 0.3 fusion.70
  183.5 0.8 copy-done.4
  184.3 0.2 copy-done.12
  184.5 5.3 %fusion = bf16[1,1536,2048]{2,1,0:T(8,128)(2,1)} fusion(bf16[256,2048]{1,0:T(8,128)(2,1)S(1)} %get-tuple-element.21, bf16[256,2048]{1,0:T(8,128)(2,1)S(1)} %get-tuple-element.22, bf16[256,1536]{1,0:T(8,128)(2,1)S(1)} %copy-done.4, bf16[256,1536]{1,0:T(8,128)(2,1)S(1)} %copy-done.12), kind=kOutput, calls=%fused_computation.1 | convolution fusion | flops 3231711232 | bytes 9961472 | tf_op jit(solution)/shard_map/dot_general | solution.py:294
  190.0 1.4 reduce_sum.58
  191.4 1.4 reduce_sum.61
  192.8 0.7 pad_maximum_fusion
  193.5 14.2 %all-to-all-done.2 = bf16[16,16,2048]{2,1,0:T(8,128)(2,1)} async-done(((bf16[16,16,2048]{2,1,0:T(8,128)(2,1)}), bf16[16,16,2048]{2,1,0:T(8,128)(2,1)}, u32[]{:S(2)}, u32[]{:S(2)}) %all-to-all-start.2) | async-done | bytes 1048608 | tf_op jit(solution)/shard_map/all_to_all | solution.py:233
  207.6 1.4 reduce_sum.60
  209.0 0.7 pad_maximum_fusion.1
  (48 shorter events, 0.5 us)
Async XLA Ops:
  25.6 6.6 %slice-start = ((s8[6291456]{0:T(1024)(128)(4,1)}), s8[4194304]{0:T(1024)(128)(4,1)S(1)}, s32[]{:S(2)}) async-start(s8[6291456]{0:T(1024)(128)(4,1)} %bitcast.91), calls=%async_computation.4 | async-start | bytes 8388608
  27.4 4.8 %slice-start.1 = ((s8[6291456]{0:T(1024)(128)(4,1)}), s8[2097152]{0:T(1024)(128)(4,1)S(1)}, s32[]{:S(2)}) async-start(s8[6291456]{0:T(1024)(128)(4,1)} %bitcast.91), calls=%async_computation.5 | async-start | bytes 4194304
  27.5 8.7 %slice-start.2 = ((s8[6291456]{0:T(1024)(128)(4,1)}), s8[4194304]{0:T(1024)(128)(4,1)S(1)}, s32[]{:S(2)}) async-start(s8[6291456]{0:T(1024)(128)(4,1)} %bitcast.93), calls=%async_computation.6 | async-start | bytes 8388608
  32.2 38.6 %copy-start.1 = (bf16[256,1536]{1,0:T(8,128)(2,1)}, bf16[256,1536]{1,0:T(8,128)(2,1)S(1)}, u32[]{:S(2)}) copy-start(bf16[256,1536]{1,0:T(8,128)(2,1)S(1)} %fusion.52) | copy-start | bytes 2359300
  32.2 4.0 %slice-start.3 = ((s8[6291456]{0:T(1024)(128)(4,1)}), s8[2097152]{0:T(1024)(128)(4,1)S(1)}, s32[]{:S(2)}) async-start(s8[6291456]{0:T(1024)(128)(4,1)} %bitcast.93), calls=%async_computation.7 | async-start | bytes 4194304
  34.9 33.4 %collective-permute-start.2 = (bf16[256,1536]{1,0:T(8,128)(2,1)S(1)}, bf16[256,1536]{1,0:T(8,128)(2,1)S(1)}, u32[]{:S(2)}, u32[]{:S(2)}) collective-permute-start(bf16[256,1536]{1,0:T(8,128)(2,1)S(1)} %fusion.52), channel_id=1, source_target_pairs={{0,16},{16,0},{1,17},{17,1},{2,18},{18,2},{3,19},{19,3},{4,20},{20... | collective-permute-start | bytes 2359304 | tf_op jit(solution)/shard_map/ppermute | solution.py:240
  38.0 32.8 %copy-start.7 = (bf16[256,1536]{1,0:T(8,128)(2,1)}, bf16[256,1536]{1,0:T(8,128)(2,1)S(1)}, u32[]{:S(2)}) copy-start(bf16[256,1536]{1,0:T(8,128)(2,1)S(1)} %fusion.58) | copy-start | bytes 2359300
  38.0 4.4 %copy-start.13 = (f32[16,32,128]{2,1,0:T(8,128)S(1)}, f32[16,32,128]{2,1,0:T(8,128)}, u32[]{:S(2)}) copy-start(f32[16,32,128]{2,1,0:T(8,128)} %get-tuple-element.10) | copy-start | bytes 786436
  38.0 32.8 %collective-permute-start.3 = (bf16[256,1536]{1,0:T(8,128)(2,1)S(1)}, bf16[256,1536]{1,0:T(8,128)(2,1)S(1)}, u32[]{:S(2)}, u32[]{:S(2)}) collective-permute-start(bf16[256,1536]{1,0:T(8,128)(2,1)S(1)} %fusion.58), channel_id=1, source_target_pairs={{0,16},{16,0},{1,17},{17,1},{2,18},{18,2},{3,19},{19,3},{4,20},{20... | collective-permute-start | bytes 2359304 | tf_op jit(solution)/shard_map/ppermute | solution.py:240
  38.3 56.9 %collective-permute-start = (bf16[256,1536]{1,0:T(8,128)(2,1)}, bf16[256,1536]{1,0:T(8,128)(2,1)}, u32[]{:S(2)}, u32[]{:S(2)}) collective-permute-start(bf16[256,1536]{1,0:T(8,128)(2,1)} %fusion.49), channel_id=1, source_target_pairs={{0,16},{16,0},{1,17},{17,1},{2,18},{18,2},{3,19},{19,3},{4,20},{20... | collective-permute-start | bytes 2359304 | tf_op jit(solution)/shard_map/ppermute | solution.py:240
  42.2 62.4 %collective-permute-start.1 = (bf16[256,1536]{1,0:T(8,128)(2,1)}, bf16[256,1536]{1,0:T(8,128)(2,1)}, u32[]{:S(2)}, u32[]{:S(2)}) collective-permute-start(bf16[256,1536]{1,0:T(8,128)(2,1)} %fusion.55), channel_id=1, source_target_pairs={{0,16},{16,0},{1,17},{17,1},{2,18},{18,2},{3,19},{19,3},{4,20},{20... | collective-permute-start | bytes 2359304 | tf_op jit(solution)/shard_map/ppermute | solution.py:240
  68.4 3.1 %copy-start.5 = (bf16[256,1536]{1,0:T(8,128)(2,1)}, bf16[256,1536]{1,0:T(8,128)(2,1)S(1)}, u32[]{:S(2)}) copy-start(bf16[256,1536]{1,0:T(8,128)(2,1)S(1)} %collective-permute-done.2) | copy-start | bytes 2359300
  70.8 0.9 copy-start.9
  71.7 5.8 %copy-start.3 = (bf16[256,1536]{1,0:T(8,128)(2,1)}, bf16[256,1536]{1,0:T(8,128)(2,1)S(1)}, u32[]{:S(2)}) copy-start(bf16[256,1536]{1,0:T(8,128)(2,1)S(1)} %multiply_convert_fusion.6) | copy-start | bytes 2359300
  77.5 9.4 %copy-start = (bf16[16,32,2048]{2,1,0:T(8,128)(2,1)S(1)}, bf16[16,32,2048]{2,1,0:T(8,128)(2,1)}, u32[]{:S(2)}) copy-start(bf16[16,32,2048]{2,1,0:T(8,128)(2,1)} %shard_map.95) | copy-start | bytes 6291460
  77.5 36.0 %all-to-all-start.1 = ((bf16[16,16,2048]{2,1,0:T(8,128)(2,1)}), bf16[16,16,2048]{2,1,0:T(8,128)(2,1)S(1)}, u32[]{:S(2)}, u32[]{:S(2)}) async-start(bf16[16,16,2048]{2,1,0:T(8,128)(2,1)} %bitcast.84), calls=%async_computation.1 | async-start | bytes 2097152 | tf_op jit(solution)/shard_map/all_to_all | solution.py:233
  93.8 36.2 %collective-permute-start.5 = (bf16[256,1536]{1,0:T(8,128)(2,1)}, bf16[256,1536]{1,0:T(8,128)(2,1)}, u32[]{:S(2)}, u32[]{:S(2)}) collective-permute-start(bf16[256,1536]{1,0:T(8,128)(2,1)} %fusion.64), channel_id=1, source_target_pairs={{0,16},{16,0},{1,17},{17,1},{2,18},{18,2},{3,19},{19,3},{4,20},{20... | collective-permute-start | bytes 2359304 | tf_op jit(solution)/shard_map/ppermute | solution.py:240
  107.1 0.9 copy-start.11
  113.5 34.6 %all-to-all-start = ((bf16[16,16,2048]{2,1,0:T(8,128)(2,1)}), bf16[16,16,2048]{2,1,0:T(8,128)(2,1)}, u32[]{:S(2)}, u32[]{:S(2)}) async-start(bf16[16,16,2048]{2,1,0:T(8,128)(2,1)} %bitcast.82), calls=%async_computation | async-start | bytes 2097152 | tf_op jit(solution)/shard_map/all_to_all | solution.py:233
  122.8 7.2 %copy-start.2 = (bf16[256,1536]{1,0:T(8,128)(2,1)S(1)}, bf16[256,1536]{1,0:T(8,128)(2,1)}, u32[]{:S(2)}) copy-start(bf16[256,1536]{1,0:T(8,128)(2,1)} %copy-done.1) | copy-start | bytes 2359300
  122.8 7.2 %copy-start.6 = (bf16[256,1536]{1,0:T(8,128)(2,1)S(1)}, bf16[256,1536]{1,0:T(8,128)(2,1)}, u32[]{:S(2)}) copy-start(bf16[256,1536]{1,0:T(8,128)(2,1)} %copy-done.5) | copy-start | bytes 2359300
  122.8 7.2 %copy-start.8 = (bf16[256,1536]{1,0:T(8,128)(2,1)S(1)}, bf16[256,1536]{1,0:T(8,128)(2,1)}, u32[]{:S(2)}) copy-start(bf16[256,1536]{1,0:T(8,128)(2,1)} %copy-done.7) | copy-start | bytes 2359300
  122.8 7.2 %copy-start.10 = (bf16[256,1536]{1,0:T(8,128)(2,1)S(1)}, bf16[256,1536]{1,0:T(8,128)(2,1)}, u32[]{:S(2)}) copy-start(bf16[256,1536]{1,0:T(8,128)(2,1)} %copy-done.9) | copy-start | bytes 2359300
  122.8 13.0 %slice-start.4 = ((s8[6291456]{0:T(1024)(128)(4,1)}), s8[4194304]{0:T(1024)(128)(4,1)S(1)}, s32[]{:S(2)}) async-start(s8[6291456]{0:T(1024)(128)(4,1)} %bitcast.95), calls=%async_computation.8 | async-start | bytes 8388608
  128.8 7.0 %slice-start.5 = ((s8[6291456]{0:T(1024)(128)(4,1)}), s8[2097152]{0:T(1024)(128)(4,1)S(1)}, s32[]{:S(2)}) async-start(s8[6291456]{0:T(1024)(128)(4,1)} %bitcast.95), calls=%async_computation.9 | async-start | bytes 4194304
  128.8 23.9 %collective-permute-start.4 = (bf16[256,1536]{1,0:T(8,128)(2,1)}, bf16[256,1536]{1,0:T(8,128)(2,1)}, u32[]{:S(2)}, u32[]{:S(2)}) collective-permute-start(bf16[256,1536]{1,0:T(8,128)(2,1)} %fusion.61), channel_id=1, source_target_pairs={{0,16},{16,0},{1,17},{17,1},{2,18},{18,2},{3,19},{19,3},{4,20},{20... | collective-permute-start | bytes 2359304 | tf_op jit(solution)/shard_map/ppermute | solution.py:240
  148.1 29.6 %all-to-all-start.3 = ((bf16[16,16,2048]{2,1,0:T(8,128)(2,1)}), bf16[16,16,2048]{2,1,0:T(8,128)(2,1)}, u32[]{:S(2)}, u32[]{:S(2)}) async-start(bf16[16,16,2048]{2,1,0:T(8,128)(2,1)} %bitcast.83), calls=%async_computation.3 | async-start | bytes 2097152 | tf_op jit(solution)/shard_map/all_to_all | solution.py:233
  177.7 29.9 %all-to-all-start.2 = ((bf16[16,16,2048]{2,1,0:T(8,128)(2,1)}), bf16[16,16,2048]{2,1,0:T(8,128)(2,1)}, u32[]{:S(2)}, u32[]{:S(2)}) async-start(bf16[16,16,2048]{2,1,0:T(8,128)(2,1)} %bitcast.81), calls=%async_computation.2 | async-start | bytes 2097152 | tf_op jit(solution)/shard_map/all_to_all | solution.py:233
  183.2 1.1 copy-start.4
  183.2 1.4 copy-start.12

commit v3 on v2

--- a/solution.py
+++ b/solution.py
@@ -229,11 +229,96 @@
     )(*blocks)
 
 
-def scatter_sum(rows):
-    parts = lax.all_to_all(
-        rows.reshape(lax.axis_size("expert"), -1, rows.shape[1]), "expert", 0, 0, tiled=True
-    )
-    return jnp.sum(parts.astype(jnp.float32), axis=0).astype(jnp.bfloat16)
+def scatter_kernel(depth, count, *refs):
+    ins, outs, rest = refs[:count], refs[count : 2 * count], refs[2 * count :]
+    from_core, core_sum, from_x, x_sum, from_z, send_sem, recv_sem = rest
+    me, piece = lax.axis_index("expert"), lax.axis_index("dp")
+    z, x, core = me // 4, (me // 2) % 2, me % 2
+    f32 = jnp.float32
+
+    def place(z_at, x_at, core_at):
+        return (z_at * 2 + x_at) * 2 + core_at
+
+    across, sibling = place(z, 1 - x, core), place(z, x, 1 - core)
+    along = [place(lax.rem(z + k, depth), x, core) for k in range(1, depth)]
+    barrier = pltpu.get_barrier_semaphore()
+    for peer in [*along, across, sibling]:
+        pl.semaphore_signal(
+            barrier, inc=1, device_id=(piece, peer), device_id_type=pl.DeviceIdType.MESH
+        )
+    pl.semaphore_wait(barrier, depth + 1)
+
+    def copy(a, src, dst, sem, peer):
+        made = pltpu.make_async_remote_copy(
+            src_ref=src,
+            dst_ref=dst,
+            send_sem=send_sem.at[a, sem],
+            recv_sem=recv_sem.at[a, sem],
+            device_id=(piece, peer),
+            device_id_type=pl.DeviceIdType.MESH,
+        )
+        made.start()
+        return made
+
+    core_step = [
+        copy(a, ins[a].at[:, :, 1 - core], from_core.at[a], 0, sibling) for a in range(count)
+    ]
+    x_step, z_step = [], []
+    for a in range(count):
+        core_step[a].wait_recv()
+
+        @pl.loop(0, depth)
+        def _(k):
+            core_sum[a, k] = (
+                ins[a][k, :, core].astype(f32) + from_core[a, k].astype(f32)
+            ).astype(jnp.bfloat16)
+
+        x_step.append(copy(a, core_sum.at[a, :, 1 - x], from_x.at[a], 1, across))
+    for a in range(count):
+        x_step[a].wait_recv()
+
+        @pl.loop(0, depth)
+        def _(k):
+            x_sum[a, k] = (
+                core_sum[a, k, x].astype(f32) + from_x[a, k].astype(f32)
+            ).astype(jnp.bfloat16)
+
+        for k in range(1, depth):
+            target = x_sum.at[a, lax.rem(z + k, depth)]
+            z_step.append(copy(a, target, from_z.at[a, k - 1], 1 + k, along[k - 1]))
+    for a in range(count):
+        total = x_sum[a, z].astype(f32)
+        for k in range(depth - 1):
+            z_step[a * (depth - 1) + k].wait_recv()
+            total = total + from_z[a, k].astype(f32)
+        outs[a][...] = total.astype(jnp.bfloat16)
+    for made in [*core_step, *x_step, *z_step]:
+        made.wait_send()
+
+
+def scatter_sum(number, *blocks):
+    experts = lax.axis_size("expert")
+    depth, count = experts // 4, len(blocks)
+    rows, width = blocks[0].shape[0] // experts, blocks[0].shape[1]
+    b16 = jnp.bfloat16
+    return pl.pallas_call(
+        functools.partial(scatter_kernel, depth, count),
+        out_shape=[jax.ShapeDtypeStruct((rows, width), b16)] * count,
+        in_specs=[pl.BlockSpec(memory_space=pltpu.VMEM)] * count,
+        out_specs=[pl.BlockSpec(memory_space=pltpu.VMEM)] * count,
+        scratch_shapes=[
+            pltpu.VMEM((count, depth, 2, rows, width), b16),
+            pltpu.VMEM((count, depth, 2, rows, width), b16),
+            pltpu.VMEM((count, depth, rows, width), b16),
+            pltpu.VMEM((count, depth, rows, width), b16),
+            pltpu.VMEM((count, depth - 1, rows, width), b16),
+            pltpu.SemaphoreType.DMA((count, depth + 1)),
+            pltpu.SemaphoreType.DMA((count, depth + 1)),
+        ],
+        compiler_params=pltpu.CompilerParams(
+            collective_id=number, has_side_effects=True, vmem_limit_bytes=24 << 20
+        ),
+    )(*[b.reshape(depth, 2, 2, rows, width) for b in blocks])
 
 
 def swap_pieces(block):
@@ -267,30 +352,37 @@
     cotangent, *gate_parts = lax.optimization_barrier((cotangent, *gate_parts))
     (all_dy,) = gather_rows(1, cotangent)
     cs = [part(all_dy, c) for c in range(chunks)]
-    hiddens, dys, mixed, token_grad = [], [], [], []
+    gate_others = [swap_pieces(p) for p in gate_parts]
+    up_parts = [
+        jnp.dot(x, up_local, preferred_element_type=f32).astype(jnp.bfloat16) for x in xs
+    ]
+    up_others = [swap_pieces(p) for p in up_parts]
+    dys = [(r.astype(f32) * w).astype(jnp.bfloat16) for r, w in zip(cs, ws)]
+    back_parts = [
+        lax.dot_general(r, down_local, last, preferred_element_type=f32).astype(jnp.bfloat16)
+        for r in dys
+    ]
+    back_others = [swap_pieces(p) for p in back_parts]
+    held = back_parts
     for c in range(chunks):
-        rows_x = xs[c]
-        gate_part = gate_parts[c]
-        gate_other = swap_pieces(gate_part)
-        up_part = jnp.dot(rows_x, up_local, preferred_element_type=f32).astype(jnp.bfloat16)
-        up_other = swap_pieces(up_part)
-        rows_dy = (cs[c].astype(f32) * ws[c]).astype(jnp.bfloat16)
-        back_part = lax.dot_general(rows_dy, down_local, last, preferred_element_type=f32).astype(
-            jnp.bfloat16
-        )
-        back_other = swap_pieces(back_part)
+        gate_others[c], up_others[c], held = lax.optimization_barrier(
+            (gate_others[c], up_others[c], held)
+        )
+    hiddens, outs, grads = [], [], []
+    for c in range(chunks):
         hidden, grad_gate, grad_up = pointwise(
-            gate_part.astype(f32) + gate_other.astype(f32),
-            up_part.astype(f32) + up_other.astype(f32),
-            back_part.astype(f32) + back_other.astype(f32),
+            gate_parts[c].astype(f32) + gate_others[c].astype(f32),
+            up_parts[c].astype(f32) + up_others[c].astype(f32),
+            held[c].astype(f32) + back_others[c].astype(f32),
         )
         out = jnp.dot(hidden, down_local, preferred_element_type=f32)
-        mixed.append(scatter_sum((out * ws[c]).astype(jnp.bfloat16)))
         grad = lax.dot_general(grad_gate, gate_local, last, preferred_element_type=f32)
         grad = grad + lax.dot_general(grad_up, up_local, last, preferred_element_type=f32)
-        token_grad.append(scatter_sum(grad.astype(jnp.bfloat16)))
+        outs.append((out * ws[c]).astype(jnp.bfloat16))
+        grads.append(grad.astype(jnp.bfloat16))
         hiddens.append(hidden)
-        dys.append(rows_dy)
+    mixed = scatter_sum(2, *outs)
+    token_grad = scatter_sum(3, *grads)
     down_grad = lax.dot_general(
         jnp.concatenate(hiddens, axis=0),
         jnp.concatenate(dys, axis=0),

time: 210 us -> 206 us (0.981)
  Pallas kernels: 49.2 us -> 101 us
  starting transfers between devices: 33.8 us -> 4.53 us
  matrix products: 63.7 us -> 46.5 us
  waiting for transfers between devices: 45.4 us -> 35.4 us
  local copies, waits for them, and re-layouts: 5.17 us -> 3.03 us
    pallas_call x0 -> x2, Pallas kernels: none -> 51.8 us  [scatter_sum(): pl.pallas_call(functools.partial(scatter_kernel, depth, count), out_shape...]
    all_to_all x4 -> x0, waiting for transfers between devices: 33.5 us -> none  [scatter_sum(): lax.all_to_all(rows.reshape(lax.axis_size('expert'), -1, rows.shape[1]),...]
    all_to_all x4 -> x0, starting transfers between devices: 28.3 us -> none  [scatter_sum(): lax.all_to_all(rows.reshape(lax.axis_size('expert'), -1, rows.shape[1]),...]
    ppermute x6, waiting for transfers between devices: 11.9 us -> 35.4 us  [swap_pieces(): return lax.ppermute(block, 'dp', [(0, 1), (1, 0)])]
    dot_general x2, matrix products: 11.4 us -> 3.79 us  [shards_dense(): out = jnp.dot(hidden, down_local, preferred_element_type=f32)]
    reduce_sum x4 -> x0, other arithmetic: 4.28 us -> none  [scatter_sum(): return jnp.sum(parts.astype(jnp.float32), axis=0).astype(jnp.bfloat16)]
    dot_general x2, matrix products: 11.3 us -> 7.21 us  [shards_dense(): lax.dot_general(grad_up, up_local, last, preferred_element_type=f32)]
    convert_element_type x3, other arithmetic: 2.1 us -> 5.95 us  [shards_dense(): dys = [(r.astype(f32) * w).astype(jnp.bfloat16) for r, w in zip(cs, ws)]]
  transfers between devices with their start and end apart: 10 -> 6, of which waited for: 5 -> 3; matrix products, arithmetic and copies ran while one was open for 31% -> 19% of each run, Pallas kernels for 12% -> 13%
where the time goes in v3:
time: 206 us; the launch traced here: 204 us
  Pallas kernels  101 us (49%)
  matrix products  46.5 us (23%)
  waiting for transfers between devices  35.4 us (17%)
  other arithmetic  12.3 us (6%)
  starting transfers between devices  4.53 us (2%)
  local copies, waits for them, and re-layouts  3.03 us (1%)
    pallas_call x2, Pallas kernels, scatter_sum(): pl.pallas_call(functools.partial(scatter_kernel, depth, count), out_shape...  51.8 us
    pallas_call x2, Pallas kernels, gather_rows(): pl.pallas_call(functools.partial(gather_kernel, depth, count), out_shape=...  49.1 us
    ppermute x6, waiting for transfers between devices, swap_pieces(): return lax.ppermute(block, 'dp', [(0, 1), (1, 0)])  35.4 us
    dot_general x2, matrix products, shards_dense(): lax.dot_general(grad_gate, gate_local, last, preferred_element_type=f32)  8.87 us
    dot_general x2, matrix products, shards_dense(): lax.dot_general(r, down_local, last, preferred_element_type=f32)  8.45 us
    dot_general x2, matrix products, shards_dense(): jnp.dot(x, gate_local, preferred_element_type=f32).astype(jnp.bfloat16)  7.41 us
    dot_general x2, matrix products, shards_dense(): lax.dot_general(grad_up, up_local, last, preferred_element_type=f32)  7.21 us
    convert_element_type x3, other arithmetic, shards_dense(): dys = [(r.astype(f32) * w).astype(jnp.bfloat16) for r, w in zip(cs, ws)]  5.95 us
  transfers between devices with their start and end apart: 6, of which 3 were waited for; matrix products, arithmetic and copies ran while one was open for 19% of the time, Pallas kernels for 13%

profile of v3, /device:TPU:11, one launch (start us, length us, event | category | flops | bytes accessed | tf_op | source)
XLA Modules:
  0.0 203.6 jit_solution(17221859993997017080)
XLA Ops:
  0.6 0.7 select_reduce_fusion
  1.4 0.1 copy.14
  1.4 0.6 pad.4.refs_1_
  2.0 23.5 %shard_map.94 = (bf16[16,32,2048]{2,1,0:T(8,128)(2,1)}, f32[16,32,128]{2,1,0:T(8,128)}) custom-call(bf16[32,2048]{1,0:T(8,128)(2,1)} %refs_0_.1, f32[32,128]{1,0:T(8,128)} %pad.4.refs_1_), custom_call_target="tpu_custom_call" | custom-call | bytes 37748736 | tf_op jit(solution)/shard_map/pallas_call | solution.py:217
  25.6 0.0 slice-start.4
  25.6 1.8 fusion.86
  27.4 0.0 slice-start.5
  27.5 0.0 slice-start.8
  27.5 5.6 %fusion.49 = bf16[256,1536]{1,0:T(8,128)(2,1)} fusion(bf16[256,2048]{1,0:T(8,128)(2,1)S(1)} %bitcast.85, bf16[1,2048,1536]{2,1,0:T(8,128)(2,1)} %param.11), kind=kOutput, calls=%fused_computation.34 | convolution fusion | flops 1611005952 | bytes 8126464 | tf_op jit(solution)/shard_map/dot_general | solution.py:350
  33.1 1.8 fusion.52
  34.9 1.3 collective-permute-start
  36.2 0.2 collective-permute-start.2
  36.4 2.7 %fusion.58 = bf16[256,1536]{1,0:T(8,128)(2,1)} fusion(bf16[256,2048]{1,0:T(8,128)(2,1)S(1)} %bitcast.88, bf16[1,2048,1536]{2,1,0:T(8,128)(2,1)S(1)} %bitcast.100), kind=kOutput, calls=%fused_computation.37 | convolution fusion | flops 1611005952 | bytes 8126464 | tf_op jit(solution)/shard_map/dot_general | solution.py:357
  39.1 1.2 collective-permute-start.3
  40.4 2.7 %fusion.55 = bf16[256,1536]{1,0:T(8,128)(2,1)} fusion(bf16[256,2048]{1,0:T(8,128)(2,1)S(1)} %bitcast.86, bf16[1,2048,1536]{2,1,0:T(8,128)(2,1)S(1)} %bitcast.100), kind=kOutput, calls=%fused_computation.36 | convolution fusion | flops 1611005952 | bytes 8126464 | tf_op jit(solution)/shard_map/dot_general | solution.py:357
  43.1 0.2 collective-permute-start.1
  43.3 25.6 %shard_map.95 = bf16[16,32,2048]{2,1,0:T(8,128)(2,1)} custom-call(bf16[32,2048]{1,0:T(8,128)(2,1)} %refs_0_.2), custom_call_target="tpu_custom_call" | custom-call | bytes 33554432 | tf_op jit(solution)/shard_map/pallas_call | solution.py:217
  68.9 0.2 dynamic-slice_reduce_fusion
  69.2 0.0 slice-start
  69.2 2.1 %multiply_convert_fusion = (bf16[16,16,2048]{2,1,0:T(8,128)(2,1)S(1)}, bf16[16,16,2048]{2,1,0:T(8,128)(2,1)S(1)}) fusion(f32[16,16]{1,0:T(8,128)S(1)} %get-tuple-element.37, bf16[16,32,2048]{2,1,0:T(8,128)(2,1)} %shard_map.95, f32[16,16]{1,0:T(8,128)S(1)} %get-tuple-element.38), kind=kLoop, calls=%fused_computation.47 | loop fusion | flops 3145728 | bytes 4196352 | tf_op jit(solution)/shard_map/convert_element_type | solution.py:360
  71.3 0.0 slice-start.1
  71.3 5.7 %fusion.61 = bf16[256,1536]{1,0:T(8,128)(2,1)} fusion(bf16[256,2048]{1,0:T(8,128)(2,1)S(1)} %bitcast.90, bf16[1,1536,2048]{2,1,0:T(8,128)(2,1)} %param.13), kind=kOutput, calls=%fused_computation.38 | convolution fusion | flops 1611005952 | bytes 8126464 | tf_op jit(solution)/shard_map/dot_general | solution.py:362
  77.0 1.2 collective-permute-start.4
  78.3 2.7 %fusion.64 = bf16[256,1536]{1,0:T(8,128)(2,1)} fusion(bf16[256,2048]{1,0:T(8,128)(2,1)S(1)} %bitcast.89, bf16[1,1536,2048]{2,1,0:T(8,128)(2,1)S(1)} %bitcast.92), kind=kOutput, calls=%fused_computation.39 | convolution fusion | flops 1611005952 | bytes 8126464 | tf_op jit(solution)/shard_map/dot_general | solution.py:362
  81.0 1.8 slice_convert_fusion.1
  82.9 0.1 mul.101
  82.9 0.1 mul.96
  83.0 2.0 fusion.70
  85.1 0.3 collective-permute-start.5
  85.4 19.5 %collective-permute-done.1 = bf16[256,1536]{1,0:T(8,128)(2,1)} collective-permute-done((bf16[256,1536]{1,0:T(8,128)(2,1)}, bf16[256,1536]{1,0:T(8,128)(2,1)}, u32[]{:S(2)}, u32[]{:S(2)}) %collective-permute-start.1) | collective-permute-done | bytes 786464 | tf_op jit(solution)/shard_map/ppermute | solution.py:325
  104.9 2.2 %multiply_convert_fusion.6 = bf16[256,1536]{1,0:T(8,128)(2,1)S(1)} fusion(bf16[256,1536]{1,0:T(8,128)(2,1)} %collective-permute-done.3, bf16[256,1536]{1,0:T(8,128)(2,1)} %fusion.58, bf16[256,1536]{1,0:T(8,128)(2,1)} %collective-permute-done.2, bf16[256,1536]{1,0:T(8,128)(2,1)S(1)} %fusion.52), kind=kLoop, calls=%fused_computation.58 | loop fusion | flops 4718592 | bytes 3932160 | tf_op jit(solution)/shard_map/convert_element_type | solution.py:14
  107.1 2.7 %multiply_convert_fusion.7 = bf16[256,1536]{1,0:T(8,128)(2,1)S(1)} fusion(bf16[256,1536]{1,0:T(8,128)(2,1)} %collective-permute-done.1, bf16[256,1536]{1,0:T(8,128)(2,1)} %fusion.55, bf16[256,1536]{1,0:T(8,128)(2,1)} %collective-permute-done, bf16[256,1536]{1,0:T(8,128)(2,1)} %fusion.49), kind=kLoop, calls=%fused_computation.63 | loop fusion | flops 4718592 | bytes 3932160 | tf_op jit(solution)/shard_map/convert_element_type | solution.py:14
  109.8 0.0 slice-start.6
  109.8 1.9 fusion.46
  111.7 0.0 slice-start.7
  111.7 0.0 slice-start.10
  111.7 1.9 fusion.43
  113.7 0.0 slice-start.11
  113.7 8.0 %collective-permute-done.4 = bf16[256,1536]{1,0:T(8,128)(2,1)} collective-permute-done((bf16[256,1536]{1,0:T(8,128)(2,1)}, bf16[256,1536]{1,0:T(8,128)(2,1)}, u32[]{:S(2)}, u32[]{:S(2)}) %collective-permute-start.4) | collective-permute-done | bytes 786464 | tf_op jit(solution)/shard_map/ppermute | solution.py:325
  121.7 4.8 %fusion.19 = f32[256,2048]{1,0:T(8,128)S(1)} fusion(bf16[1,2048,1536]{2,1,0:T(8,128)(2,1)S(1)} %bitcast.98, bf16[256,1536]{1,0:T(8,128)(2,1)} %collective-permute-done, bf16[256,1536]{1,0:T(8,128)(2,1)} %fusion.49, bf16[256,1536]{1,0:T(8,128)(2,1)} %collective-permute-done.1, bf16[256,1536]{1,0:T(8,128)(2,1)} %fusion.55, ...), kind=kOutput, calls=%fused_computation.20 | convolution fusion | flops 1618083840 | bytes 13107200 | tf_op jit(solution)/shard_map/dot_general | solution.py:379
  126.6 4.0 %fusion.40 = bf16[256,2048]{1,0:T(8,128)(2,1)S(1)} fusion(f32[256,2048]{1,0:T(8,128)S(1)} %fusion.19, bf16[1,2048,1536]{2,1,0:T(8,128)(2,1)S(1)} %bitcast.102, bf16[256,1536]{1,0:T(8,128)(2,1)} %collective-permute-done.4, bf16[256,1536]{1,0:T(8,128)(2,1)} %fusion.61, bf16[256,1536]{1,0:T(8,128)(2,1)} %collective-permute-done, bf16[256,1536]{1,0:T(8,128)(2,1)} %fusion.49), kind=kOutput, calls=%fused_computation.31 | convolution fusion | flops 1616379904 | bytes 12582912 | tf_op jit(solution)/shard_map/dot_general | solution.py:380
  130.5 7.9 %collective-permute-done.5 = bf16[256,1536]{1,0:T(8,128)(2,1)S(1)} collective-permute-done((bf16[256,1536]{1,0:T(8,128)(2,1)S(1)}, bf16[256,1536]{1,0:T(8,128)(2,1)S(1)}, u32[]{:S(2)}, u32[]{:S(2)}) %collective-permute-start.5) | collective-permute-done | bytes 786464 | tf_op jit(solution)/shard_map/ppermute | solution.py:325
  138.5 4.1 %fusion.17 = f32[256,2048]{1,0:T(8,128)S(1)} fusion(bf16[1,2048,1536]{2,1,0:T(8,128)(2,1)S(1)} %bitcast.98, bf16[256,1536]{1,0:T(8,128)(2,1)} %collective-permute-done.2, bf16[256,1536]{1,0:T(8,128)(2,1)S(1)} %fusion.52, bf16[256,1536]{1,0:T(8,128)(2,1)} %collective-permute-done.3, bf16[256,1536]{1,0:T(8,128)(2,1)} %fusion.58, ...), kind=kOutput, calls=%fused_computation.18 | convolution fusion | flops 1618083840 | bytes 13107200 | tf_op jit(solution)/shard_map/dot_general | solution.py:379
  142.5 3.2 %fusion.37 = bf16[256,2048]{1,0:T(8,128)(2,1)S(1)} fusion(f32[256,2048]{1,0:T(8,128)S(1)} %fusion.17, bf16[1,2048,1536]{2,1,0:T(8,128)(2,1)S(1)} %bitcast.102, bf16[256,1536]{1,0:T(8,128)(2,1)S(1)} %collective-permute-done.5, bf16[256,1536]{1,0:T(8,128)(2,1)S(1)} %copy-done.2, bf16[256,1536]{1,0:T(8,128)(2,1)} %collective-permute-done.2, ...), kind=kOutput, calls=%fused_computation.30 | convolution fusion | flops 1616379904 | bytes 12582912 | tf_op jit(solution)/shard_map/dot_general | solution.py:380
  145.8 27.4 %shard_map.97 = (bf16[16,2048]{1,0:T(8,128)(2,1)S(1)}, bf16[16,2048]{1,0:T(8,128)(2,1)S(1)}) custom-call(bf16[4,2,2,16,2048]{4,3,2,1,0:T(8,128)(2,1)S(1)} %bitcast.83, bf16[4,2,2,16,2048]{4,3,2,1,0:T(8,128)(2,1)S(1)} %bitcast.84), custom_call_target="tpu_custom_call" | custom-call | tf_op jit(solution)/shard_map/pallas_call | solution.py:304
  173.2 24.3 %shard_map.96 = (bf16[16,2048]{1,0:T(8,128)(2,1)S(1)}, bf16[16,2048]{1,0:T(8,128)(2,1)S(1)}) custom-call(bf16[4,2,2,16,2048]{4,3,2,1,0:T(8,128)(2,1)S(1)} %bitcast.81, bf16[4,2,2,16,2048]{4,3,2,1,0:T(8,128)(2,1)S(1)} %bitcast.82), custom_call_target="tpu_custom_call" | custom-call | tf_op jit(solution)/shard_map/pallas_call | solution.py:304
  197.5 5.4 %fusion = bf16[1,1536,2048]{2,1,0:T(8,128)(2,1)} fusion(bf16[256,2048]{1,0:T(8,128)(2,1)S(1)} %get-tuple-element.45, bf16[256,2048]{1,0:T(8,128)(2,1)S(1)} %get-tuple-element.46, bf16[256,1536]{1,0:T(8,128)(2,1)S(1)} %multiply_convert_fusion.6, bf16[256,1536]{1,0:T(8,128)(2,1)S(1)} %multiply_convert_fusion.7), kind=kOutput, calls=%fused_computation.1 | convolution fusion | flops 3231711232 | bytes 9961472 | tf_op jit(solution)/shard_map/dot_general | solution.py:386
  202.9 0.7 pad_maximum_fusion
  (30 shorter events, 0.1 us)
Async XLA Ops:
  25.6 7.5 %slice-start.4 = ((s8[6291456]{0:T(1024)(128)(4,1)}), s8[4194304]{0:T(1024)(128)(4,1)S(1)}, s32[]{:S(2)}) async-start(s8[6291456]{0:T(1024)(128)(4,1)} %bitcast.95), calls=%async_computation.4 | async-start | bytes 8388608
  27.4 5.7 %slice-start.5 = ((s8[6291456]{0:T(1024)(128)(4,1)}), s8[2097152]{0:T(1024)(128)(4,1)S(1)}, s32[]{:S(2)}) async-start(s8[6291456]{0:T(1024)(128)(4,1)} %bitcast.95), calls=%async_computation.5 | async-start | bytes 4194304
  27.5 9.0 %slice-start.8 = ((s8[6291456]{0:T(1024)(128)(4,1)}), s8[4194304]{0:T(1024)(128)(4,1)S(1)}, s32[]{:S(2)}) async-start(s8[6291456]{0:T(1024)(128)(4,1)} %bitcast.99), calls=%async_computation.8 | async-start | bytes 8388608
  33.1 3.3 %slice-start.9 = ((s8[6291456]{0:T(1024)(128)(4,1)}), s8[2097152]{0:T(1024)(128)(4,1)S(1)}, s32[]{:S(2)}) async-start(s8[6291456]{0:T(1024)(128)(4,1)} %bitcast.99), calls=%async_computation.9 | async-start | bytes 4194304
  34.9 50.2 %collective-permute-start = (bf16[256,1536]{1,0:T(8,128)(2,1)}, bf16[256,1536]{1,0:T(8,128)(2,1)}, u32[]{:S(2)}, u32[]{:S(2)}) collective-permute-start(bf16[256,1536]{1,0:T(8,128)(2,1)} %fusion.49), channel_id=1, source_target_pairs={{0,16},{16,0},{1,17},{17,1},{2,18},{18,2},{3,19},{19,3},{4,20},{20... | collective-permute-start | bytes 2359304 | tf_op jit(solution)/shard_map/ppermute | solution.py:325
  36.2 68.6 %collective-permute-start.2 = (bf16[256,1536]{1,0:T(8,128)(2,1)S(1)}, bf16[256,1536]{1,0:T(8,128)(2,1)}, u32[]{:S(2)}, u32[]{:S(2)}) collective-permute-start(bf16[256,1536]{1,0:T(8,128)(2,1)S(1)} %fusion.52), channel_id=1, source_target_pairs={{0,16},{16,0},{1,17},{17,1},{2,18},{18,2},{3,19},{19,3},{4,20},{20... | collective-permute-start | bytes 2359304 | tf_op jit(solution)/shard_map/ppermute | solution.py:325
  39.1 65.7 %collective-permute-start.3 = (bf16[256,1536]{1,0:T(8,128)(2,1)}, bf16[256,1536]{1,0:T(8,128)(2,1)}, u32[]{:S(2)}, u32[]{:S(2)}) collective-permute-start(bf16[256,1536]{1,0:T(8,128)(2,1)} %fusion.58), channel_id=1, source_target_pairs={{0,16},{16,0},{1,17},{17,1},{2,18},{18,2},{3,19},{19,3},{4,20},{20... | collective-permute-start | bytes 2359304 | tf_op jit(solution)/shard_map/ppermute | solution.py:325
  43.1 25.8 %copy-start.1 = (f32[16,32,128]{2,1,0:T(8,128)S(1)}, f32[16,32,128]{2,1,0:T(8,128)}, u32[]{:S(2)}) copy-start(f32[16,32,128]{2,1,0:T(8,128)} %get-tuple-element.23) | copy-start | bytes 786436
  43.1 61.8 %collective-permute-start.1 = (bf16[256,1536]{1,0:T(8,128)(2,1)}, bf16[256,1536]{1,0:T(8,128)(2,1)}, u32[]{:S(2)}, u32[]{:S(2)}) collective-permute-start(bf16[256,1536]{1,0:T(8,128)(2,1)} %fusion.55), channel_id=1, source_target_pairs={{0,16},{16,0},{1,17},{17,1},{2,18},{18,2},{3,19},{19,3},{4,20},{20... | collective-permute-start | bytes 2359304 | tf_op jit(solution)/shard_map/ppermute | solution.py:325
  69.2 9.1 %slice-start = ((s8[6291456]{0:T(1024)(128)(4,1)}), s8[4194304]{0:T(1024)(128)(4,1)S(1)}, s32[]{:S(2)}) async-start(s8[6291456]{0:T(1024)(128)(4,1)} %bitcast.91), calls=%async_computation | async-start | bytes 8388608
  71.3 7.0 %slice-start.1 = ((s8[6291456]{0:T(1024)(128)(4,1)}), s8[2097152]{0:T(1024)(128)(4,1)S(1)}, s32[]{:S(2)}) async-start(s8[6291456]{0:T(1024)(128)(4,1)} %bitcast.91), calls=%async_computation.1 | async-start | bytes 4194304
  77.0 44.7 %collective-permute-start.4 = (bf16[256,1536]{1,0:T(8,128)(2,1)}, bf16[256,1536]{1,0:T(8,128)(2,1)}, u32[]{:S(2)}, u32[]{:S(2)}) collective-permute-start(bf16[256,1536]{1,0:T(8,128)(2,1)} %fusion.61), channel_id=1, source_target_pairs={{0,16},{16,0},{1,17},{17,1},{2,18},{18,2},{3,19},{19,3},{4,20},{20... | collective-permute-start | bytes 2359304 | tf_op jit(solution)/shard_map/ppermute | solution.py:325
  78.3 2.7 %copy-start = (bf16[16,32,2048]{2,1,0:T(8,128)(2,1)S(1)}, bf16[16,32,2048]{2,1,0:T(8,128)(2,1)}, u32[]{:S(2)}) copy-start(bf16[16,32,2048]{2,1,0:T(8,128)(2,1)} %shard_map.95) | copy-start | bytes 6291460
  83.0 2.1 %copy-start.2 = (bf16[256,1536]{1,0:T(8,128)(2,1)S(1)}, bf16[256,1536]{1,0:T(8,128)(2,1)}, u32[]{:S(2)}) copy-start(bf16[256,1536]{1,0:T(8,128)(2,1)} %fusion.64) | copy-start | bytes 2359300
  83.0 26.8 %slice-start.2 = ((s8[6291456]{0:T(1024)(128)(4,1)}), s8[2097152]{0:T(1024)(128)(4,1)S(1)}, s32[]{:S(2)}) async-start(s8[6291456]{0:T(1024)(128)(4,1)} %bitcast.93), calls=%async_computation.2 | async-start | bytes 4194304
  85.1 24.7 %slice-start.3 = ((s8[6291456]{0:T(1024)(128)(4,1)}), s8[4194304]{0:T(1024)(128)(4,1)S(1)}, s32[]{:S(2)}) async-start(s8[6291456]{0:T(1024)(128)(4,1)} %bitcast.93), calls=%async_computation.3 | async-start | bytes 8388608
  85.1 53.4 %collective-permute-start.5 = (bf16[256,1536]{1,0:T(8,128)(2,1)S(1)}, bf16[256,1536]{1,0:T(8,128)(2,1)S(1)}, u32[]{:S(2)}, u32[]{:S(2)}) collective-permute-start(bf16[256,1536]{1,0:T(8,128)(2,1)S(1)} %copy-done.2), channel_id=1, source_target_pairs={{0,16},{16,0},{1,17},{17,1},{2,18},{18,2},{3,19},{19,3},{4,20},{20... | collective-permute-start | bytes 2359304 | tf_op jit(solution)/shard_map/ppermute | solution.py:325
  109.8 11.9 %slice-start.6 = ((s8[6291456]{0:T(1024)(128)(4,1)}), s8[4194304]{0:T(1024)(128)(4,1)S(1)}, s32[]{:S(2)}) async-start(s8[6291456]{0:T(1024)(128)(4,1)} %bitcast.97), calls=%async_computation.6 | async-start | bytes 8388608
  111.7 10.0 %slice-start.7 = ((s8[6291456]{0:T(1024)(128)(4,1)}), s8[2097152]{0:T(1024)(128)(4,1)S(1)}, s32[]{:S(2)}) async-start(s8[6291456]{0:T(1024)(128)(4,1)} %bitcast.97), calls=%async_computation.7 | async-start | bytes 4194304
  111.7 14.8 %slice-start.10 = ((s8[6291456]{0:T(1024)(128)(4,1)}), s8[4194304]{0:T(1024)(128)(4,1)S(1)}, s32[]{:S(2)}) async-start(s8[6291456]{0:T(1024)(128)(4,1)} %bitcast.101), calls=%async_computation.10 | async-start | bytes 8388608
  113.7 12.9 %slice-start.11 = ((s8[6291456]{0:T(1024)(128)(4,1)}), s8[2097152]{0:T(1024)(128)(4,1)S(1)}, s32[]{:S(2)}) async-start(s8[6291456]{0:T(1024)(128)(4,1)} %bitcast.101), calls=%async_computation.11 | async-start | bytes 4194304
